TPU v7x, 128 devices: a whole 4x4x4 slice. The times are simulated.
128 devices in a mesh: row: 16 (over y, z), col: 8 (over x, core).
Axes of the slice: x: 4, y: 4, z: 4, core: 2. Of those that a mesh axis runs over, the one named last changes fastest.
Arguments:
- ancestor_inv: float32 [24576, 24576], P('row', 'col'), may hold values from -6 to 6
- update_tiles: int32 [96], replicated, may hold values from 0 to 191, as said below
- tile_slot: int32 [192], replicated, may hold values from 0 to 191, as said below
- lower_below: float32 [12288, 1024], P('col', 'row'), may hold values from -0.078125 to 0.078125
- diag_factor: float32 [1024, 1024], replicated
Outputs:
- cov_below: float32 [12288, 1024], P('row', 'col')
- cov_diag: float32 [1024, 1024], P(None, 'col')
Inputs may be any that keep to these rules, and one draw needn't show every extreme that they name: `update_tiles`: strictly increasing; exactly 12 entries lie in each run of 24 ancestor tiles starting at a multiple of 24. `tile_slot`: A permutation; owner o holds slots 12 * o to 12 * o + 11. Of the update tiles 6 * i to 6 * i + 5, at most 1 have their slots with one owner, and exactly 1 with some owner.
All inputs are finite; a program needn't handle non-finite values.
Results may differ from a plain program's by a relative error of at most 0.000098.
Values sent between devices are 32-bit elements; how exact they have to be, the bound alone decides.
A program may use at most 192 MiB of HBM per device.

v0:
```python
import jax
import jax.numpy as jnp
from jax import lax
from jax.sharding import PartitionSpec as P

TILE = 128
ATILES = 192
UTILES = 96
JW = 1024


def spread(value, axis, root):
    mine = lax.axis_index(axis) == root
    return lax.psum(jnp.where(mine, value, jnp.zeros_like(value)), axis)


def solve_right(rows, factor):
    return jax.scipy.linalg.solve_triangular(factor, rows.T, lower=True, trans=1).T


def shards(ancestor_inv, update_tiles, tile_slot, lower_below, diag_factor):
    rows_count = lax.axis_size("row")
    cols_count = lax.axis_size("col")
    this_row = lax.axis_index("row")
    this_col = lax.axis_index("col")
    share_rows = UTILES // rows_count
    share_cols = UTILES // cols_count
    slots_dev = ATILES // rows_count
    block_cols = ATILES // cols_count
    capacity = (share_rows + rows_count - 1) // rows_count
    narrow = JW // cols_count
    exact = lax.Precision.HIGHEST
    gathered = lax.all_gather(lower_below, "row", axis=1, tiled=True)
    scaled = solve_right(gathered, diag_factor)
    positions = jnp.arange(UTILES, dtype=jnp.int32)
    slot_of = jnp.take(tile_slot, update_tiles)
    owner_of = slot_of // slots_dev
    target_of = positions // share_rows
    same_group = (
        (owner_of[:, None] == owner_of[None, :])
        & (target_of[:, None] == target_of[None, :])
        & (positions[None, :] < positions[:, None])
    )
    rank_of = jnp.sum(same_group.astype(jnp.int32), axis=1)
    send_slots = jnp.arange(rows_count * capacity, dtype=jnp.int32)
    target_ids = send_slots // capacity
    rank_ids = send_slots % capacity
    matches = (
        (target_of[None, :] == target_ids[:, None])
        & (owner_of[None, :] == this_row)
        & (rank_of[None, :] == rank_ids[:, None])
    )
    local_slot = jnp.sum(jnp.where(matches, slot_of[None, :] - this_row * slots_dev, 0), axis=1)
    present = jnp.any(matches, axis=1).astype(jnp.float32)
    col_tiles = (
        lax.dynamic_slice_in_dim(update_tiles, this_col * share_cols, share_cols)
        - this_col * block_cols
    )
    tiled = ancestor_inv.reshape(slots_dev * TILE, block_cols, TILE)
    local_cols = jnp.take(tiled, col_tiles, axis=1).reshape(slots_dev, TILE, share_cols * TILE)
    own_positions = lax.dynamic_slice_in_dim(positions, this_row * share_rows, share_rows)
    arrival = jnp.take(owner_of, own_positions) * capacity + jnp.take(rank_of, own_positions)
    outgoing = jnp.take(local_cols, local_slot, axis=0) * present[:, None, None]
    incoming = lax.all_to_all(outgoing, "row", split_axis=0, concat_axis=0, tiled=True)
    front_tiles = jnp.take(incoming, arrival, axis=0).reshape(share_rows * TILE, share_cols * TILE)
    row_terms = jnp.dot(front_tiles, scaled, precision=exact)
    cov_below = -lax.psum_scatter(row_terms, "col", scatter_dimension=1, tiled=True)
    root = this_row * share_rows // share_cols
    start = this_row * share_rows % share_cols * TILE
    own_scaled = lax.dynamic_slice_in_dim(scaled, start, share_rows * TILE, 0)
    front_scaled = spread(own_scaled, "col", root)
    columns = (
        jnp.arange(JW, dtype=jnp.int32)[:, None]
        == this_col * narrow + jnp.arange(narrow, dtype=jnp.int32)[None, :]
    ).astype(jnp.float32)
    half_solve = jax.scipy.linalg.solve_triangular(diag_factor, columns, lower=True)
    diag_inverse = jax.scipy.linalg.solve_triangular(diag_factor, half_solve, lower=True, trans=1)
    cross = lax.psum(jnp.dot(front_scaled.T, cov_below, precision=exact), "row")
    cov_diag = diag_inverse - cross
    return (cov_below, cov_diag)


def solution(mesh):
    in_specs = (P("row", "col"), P(), P(), P("col", "row"), P())
    out_specs = (P("row", "col"), P(None, "col"))
    return jax.shard_map(shards, mesh=mesh, in_specs=in_specs, out_specs=out_specs, check_vma=False)
```

profile of v0, /device:TPU:6, one launch (start us, length us, event | category | flops | bytes accessed | tf_op | source)
XLA Modules:
  0.0 579.6 jit_solution(9507025405317064819)
XLA Ops:
  7.9 18.8 %copy.11 = f32[1536,3072]{0,1:T(8,128)} copy(f32[1536,3072]{1,0:T(8,128)} %param.7) | data formatting | bytes 37748736 | tf_op args[0]
  26.7 18.7 %copy.12 = f32[1536,24,128]{2,0,1:T(8,128)} copy(f32[1536,24,128]{0,2,1:T(8,128)} %bitcast.129) | data formatting | bytes 37748736 | tf_op jit(solution)/shard_map/reshape | solution.py:59
  47.1 11.3 %gather_fusion.1 = f32[12,1536,128]{2,1,0:T(8,128)} fusion(f32[1536,24,128]{2,0,1:T(8,128)} %copy.12, s32[1024]{0:T(1024)S(1)} %get-tuple-element.67), kind=kCustom, calls=%fused_computation.3 | custom fusion | bytes 18874416 | tf_op jit(solution)/shard_map/jit(_take)/gather | solution.py:60
  58.5 12.7 %copy.13 = f32[1536,12,128]{2,1,0:T(8,128)} copy(f32[1536,12,128]{2,0,1:T(8,128)} %bitcast.130) | data formatting | bytes 18874368 | tf_op jit(solution)/shard_map/jit(_take)/gather | solution.py:60
  71.2 11.9 %gather.34 = f32[12,128,1536]{2,1,0:T(8,128)} reshape(f32[1536,12,128]{2,1,0:T(8,128)} %copy.13) | data formatting | bytes 18874368 | tf_op jit(solution)/shard_map/jit(_take)/gather | solution.py:60
  83.3 8.4 %broadcast_select_fusion = f32[12,128,1536]{2,1,0:T(8,128)} fusion(f32[12,128,1536]{2,1,0:T(8,128)} %gather.34, pred[1536]{0:T(1024)(128)(4,1)S(1)} %broadcast_bitcast_fusion), kind=kLoop, calls=%fused_computation.10 | loop fusion | flops 2359296 | bytes 18875904 | tf_op jit(solution)/shard_map/jit(_take)/select_n | solution.py:60
  91.7 9.5 %gather_fusion.2 = f32[16,128,1536]{2,1,0:T(8,128)} fusion(f32[12,128,1536]{2,1,0:T(8,128)} %broadcast_select_fusion, s32[1024]{0:T(1024)S(1)} %get-tuple-element.66), kind=kCustom, calls=%fused_computation.4 | custom fusion | bytes 25165888 | tf_op jit(solution)/shard_map/jit(_take)/gather | solution.py:63
  101.2 10.9 %select_multiply_fusion = f32[16,128,1536]{2,1,0:T(8,128)} fusion(f32[16,128,1536]{2,1,0:T(8,128)} %gather_fusion.2, f32[16]{0:T(128)S(1)} %convert_element_type.14, pred[16]{0:T(512)(128)(4,1)S(1)} %compare_and_fusion.2), kind=kLoop, calls=%fused_computation.8 | loop fusion | flops 6291456 | bytes 25165904 | tf_op jit(solution)/shard_map/mul | solution.py:63
  112.1 8.4 %all-to-all-start = ((f32[16,128,1536]{2,1,0:T(8,128)}), f32[16,128,1536]{2,1,0:T(8,128)}, u32[]{:S(2)}, u32[]{:S(2)}) async-start(f32[16,128,1536]{2,1,0:T(8,128)} %select_multiply_fusion), calls=%async_computation | async-start | bytes 25165824 | tf_op jit(solution)/shard_map/all_to_all | solution.py:64
  122.4 4.7 fusion
  127.1 22.5 %while.1 = (s32[]{:T(128)}, f32[1024,1024]{1,0:T(8,128)}, s32[8,2]{0,1:T(2,128)S(1)}, f32[8,128,128]{2,1,0:T(8,128)S(1)}, s32[]{:T(128)}) while((s32[]{:T(128)}, f32[1024,1024]{1,0:T(8,128)}, s32[8,2]{0,1:T(2,128)S(1)}, f32[8,128,128]{2,1,0:T(8,128)S(1)}, s32[]{:T(128)}) %tuple.53), condition=%wide.while_cond, body=%wide.while_body.sunk | while | flops 2 | bytes 131189 | solution.py:18
  127.7 2.2 bitcast_dynamic-update-slice_fusion.2
  130.5 2.2 bitcast_dynamic-update-slice_fusion.2
  133.3 2.2 bitcast_dynamic-update-slice_fusion.2
  136.1 2.2 bitcast_dynamic-update-slice_fusion.2
  139.0 2.2 bitcast_dynamic-update-slice_fusion.2
  141.8 2.2 bitcast_dynamic-update-slice_fusion.2
  144.6 2.2 bitcast_dynamic-update-slice_fusion.2
  147.4 2.1 bitcast_dynamic-update-slice_fusion.2
  149.6 78.6 %custom-call.10 = f32[8,128,128]{1,2,0:T(8,128)S(1)} custom-call(f32[8,128,128]{2,1,0:T(8,128)S(1)} %get-tuple-element.10), custom_call_target="InvertDiagBlocksLowerTriangular" | custom-call | tf_op jit(solution)/shard_map/jit(_solve_triangular)/triangular_solve | solution.py:18
  231.6 1.9 fusion.20
  233.6 2.2 convolution_subtract_fusion.4
  236.5 2.2 convolution_subtract_fusion
  239.6 2.5 convolution_subtract_fusion.3
  242.9 2.8 fusion.9
  246.7 3.6 convolution_subtract_fusion.2
  251.3 3.7 convolution_subtract_fusion.5
  256.2 4.2 convolution_subtract_fusion.1
  260.4 1.7 convolution_dynamic-update-slice_fusion
  268.8 68.1 %all-to-all-done = f32[16,128,1536]{2,1,0:T(8,128)} async-done(((f32[16,128,1536]{2,1,0:T(8,128)}), f32[16,128,1536]{2,1,0:T(8,128)}, u32[]{:S(2)}, u32[]{:S(2)}) %all-to-all-start) | async-done | bytes 12582944 | tf_op jit(solution)/shard_map/all_to_all | solution.py:64
  336.9 7.5 %gather_fusion.3 = f32[6,128,1536]{2,1,0:T(8,128)} fusion(f32[16,128,1536]{2,1,0:T(8,128)} %all-to-all-done, s32[1024]{0:T(1024)S(1)} %pad_clamp_fusion), kind=kCustom, calls=%fused_computation.5 | custom fusion | bytes 9437208 | tf_op jit(solution)/shard_map/jit(_take)/gather | solution.py:65
  344.4 2.7 bitcast_select_fusion
  347.2 18.4 %fusion.111 = f32[768,1024]{1,0:T(8,128)} fusion(f32[768,1536]{1,0:T(8,128)S(1)} %bitcast_select_fusion, f32[1024,1536]{1,0:T(8,128)} %constant_dynamic-update-slice_fusion.18), kind=kOutput, calls=%fused_computation.254 | convolution fusion | flops 14495514624 | bytes 14155776 | tf_op jit(solution)/shard_map/dot_general | solution.py:66
  367.4 1.3 convolution_subtract_fusion.18
  369.0 1.4 convolution_subtract_fusion.13
  370.8 1.5 convolution_subtract_fusion.12
  372.6 1.6 convolution_subtract_fusion.11
  377.5 1.4 convolution_subtract_fusion.17
  379.2 1.5 convolution_subtract_fusion.16
  381.0 1.7 convolution_subtract_fusion.8
  382.9 1.8 convolution_subtract_fusion.7
  384.8 3.8 select_bitcast_fusion
  389.0 1.9 convolution_subtract_fusion.6
  391.2 15.1 %reduce-scatter.2.cloned.1.call-done = f32[768,128]{1,0:T(8,128)} async-done(((f32[768,1024]{1,0:T(8,128)}), f32[768,128]{1,0:T(8,128)}) %reduce-scatter.2.cloned.1.call-update) | async-done | bytes 393232 | tf_op jit(solution)/shard_map/reduce_scatter | solution.py:67
  407.3 70.1 %all-reduce.3.cloned.1.call-done = f32[768,1024]{0,1:T(8,128)} async-done(((f32[768,1024]{0,1:T(8,128)}), f32[768,1024]{0,1:T(8,128)}) %all-reduce.3.cloned.1.call-update) | async-done | bytes 3145744 | tf_op jit(solution)/shard_map/psum | solution.py:14
  477.4 5.3 fusion.112
  482.8 87.9 %all-reduce.5.cloned.1.call-done = f32[1024,128]{1,0:T(8,128)} async-done(((f32[1024,128]{1,0:T(8,128)}), f32[1024,128]{1,0:T(8,128)}) %all-reduce.5.cloned.1.call-update) | async-done | bytes 524304 | tf_op jit(solution)/shard_map/psum | solution.py:78
  570.7 1.9 sub.43
  (136 shorter events, 33.1 us)
Async XLA Ops:
  7.2 38.2 %copy-start = (s32[192]{0:T(256)S(1)}, s32[192]{0:T(256)}, u32[]{:S(2)}) copy-start(s32[192]{0:T(256)} %param.9) | copy-start | bytes 2308
  7.2 224.4 %all-gather.2.cloned.1.call-start = ((), (), s32[]{:S(2)}) async-start(), calls=%async_computation.2 | async-start | bytes 6684672 | tf_op jit(solution)/shard_map/all_gather | solution.py:33
  26.7 18.7 %copy-start.4 = (s32[96]{0:T(128)S(1)}, s32[96]{0:T(128)}, u32[]{:S(2)}) copy-start(s32[96]{0:T(128)} %param.8) | copy-start | bytes 1156
  112.1 224.9 %all-to-all-start = ((f32[16,128,1536]{2,1,0:T(8,128)}), f32[16,128,1536]{2,1,0:T(8,128)}, u32[]{:S(2)}, u32[]{:S(2)}) async-start(f32[16,128,1536]{2,1,0:T(8,128)} %select_multiply_fusion), calls=%async_computation | async-start | bytes 25165824 | tf_op jit(solution)/shard_map/all_to_all | solution.py:64
  120.4 285.8 %reduce-scatter.2.cloned.1.call-start = ((), (), s32[]{:S(2)}) async-start(), calls=%async_computation.3 | async-start | bytes 3538944 | tf_op jit(solution)/shard_map/reduce_scatter | solution.py:67
  233.6 6.0 %copy-start.2 = (f32[1536,1024]{0,1:T(8,128)S(1)}, f32[1536,1024]{0,1:T(8,128)}, u32[]{:S(2)}) copy-start(f32[1536,1024]{0,1:T(8,128)} %all-gather.2.cloned.1.call-done) | copy-start | bytes 18874372
  365.6 111.9 %all-reduce.3.cloned.1.call-start = ((), (), s32[]{:S(2)}) async-start(), calls=%async_computation.4 | async-start | bytes 6291456 | tf_op jit(solution)/shard_map/psum | solution.py:14
  388.6 182.1 %all-reduce.5.cloned.1.call-start = ((), (), s32[]{:S(2)}) async-start(), calls=%async_computation.5 | async-start | bytes 1048576 | tf_op jit(solution)/shard_map/psum | solution.py:78
  388.9 183.7 %copy-start.1 = (s32[192]{0:T(256)S(1)}, s32[192]{0:T(256)}, u32[]{:S(2)}) copy-start(s32[192]{0:T(256)} %param.9) | copy-start | bytes 2308
  407.3 165.3 %copy-start.3 = (f32[768,128]{1,0:T(8,128)}, f32[768,128]{1,0:T(8,128)S(1)}, u32[]{:S(2)}) copy-start(f32[768,128]{1,0:T(8,128)S(1)} %neg.3) | copy-start | bytes 1179652
Sparse Core Ops, SparseCore 0:
  10.2 63.7 all-gather.1
  365.7 40.5 reduce-scatter.1
  408.6 68.7 all-reduce.2
  482.9 87.7 all-reduce.4
where the time goes:
time: 589 us; the launch traced here: 580 us
  waiting for transfers between devices  242 us (41%)
  local copies, waits for them, and re-layouts  123 us (21%)
  other arithmetic  113 us (19%)
  matrix products  77.1 us (13%)
  between operations  15 us (3%)
  starting transfers between devices  9.25 us (2%)
    psum x1, waiting for transfers between devices, shards(): cross = lax.psum(jnp.dot(front_scaled.T, cov_below, precision=exact), 'row')  87.9 us
    another operation x3, other arithmetic, solve_right(): jax.scipy.linalg.solve_triangular(factor, rows.T, lower=True, trans=1)  83.3 us
    psum x1, waiting for transfers between devices, spread(): return lax.psum(jnp.where(mine, value, jnp.zeros_like(value)), axis)  70.1 us
    all_to_all x1, waiting for transfers between devices, shards(): lax.all_to_all(outgoing, 'row', split_axis=0, concat_axis=0, tiled=True)  68.1 us
    gather x3, local copies, waits for them, and re-layouts, shards(): jnp.take(tiled, col_tiles, axis=1)  35.9 us
    another operation x15, matrix products, solve_right(): jax.scipy.linalg.solve_triangular(factor, rows.T, lower=True, trans=1)  29.5 us
    unnamed x47, local copies, waits for them, and re-layouts  25.3 us
    another operation x24, local copies, waits for them, and re-layouts  22.4 us
  transfers between devices with their start and end apart: 5, of which 4 were waited for; matrix products, arithmetic and copies ran while one was open for 48% of the time, Pallas kernels for 0%

commit v1 on v0

--- a/solution.py
+++ b/solution.py
@@ -1,12 +1,21 @@
 import jax
 import jax.numpy as jnp
 from jax import lax
+from jax.experimental import pallas as pl
+from jax.experimental.pallas import tpu as pltpu
 from jax.sharding import PartitionSpec as P
 
 TILE = 128
 ATILES = 192
 UTILES = 96
 JW = 1024
+MESH = pl.DeviceIdType.MESH
+F32, BF16 = jnp.float32, jnp.bfloat16
+VMEM = pl.BlockSpec(memory_space=pltpu.VMEM)
+SMEM = pl.BlockSpec(memory_space=pltpu.SMEM)
+ANY = pl.BlockSpec(memory_space=pl.ANY)
+LIMIT = 60 * 1024 * 1024
+ROWS, COLS, SLOT, FROM, OVER = 0, 8, 20, 36, 42
 
 
 def spread(value, axis, root):
@@ -18,7 +27,7 @@
     return jax.scipy.linalg.solve_triangular(factor, rows.T, lower=True, trans=1).T
 
 
-def shards(ancestor_inv, update_tiles, tile_slot, lower_below, diag_factor):
+def general(ancestor_inv, update_tiles, tile_slot, lower_below, diag_factor):
     rows_count = lax.axis_size("row")
     cols_count = lax.axis_size("col")
     this_row = lax.axis_index("row")
@@ -80,6 +89,560 @@
     return (cov_below, cov_diag)
 
 
+def split(value):
+    high = value.astype(BF16)
+    return high, (value - high.astype(F32)).astype(BF16)
+
+
+def dot3(ah, al, bh, bl):
+    out = jnp.dot(ah, bh, preferred_element_type=F32)
+    out += jnp.dot(ah, bl, preferred_element_type=F32)
+    return out + jnp.dot(al, bh, preferred_element_type=F32)
+
+
+def exact(a, b):
+    return jnp.dot(a, b, precision=lax.Precision.HIGHEST, preferred_element_type=F32)
+
+
+def remote(src, dst, send, recv, row, col):
+    return pltpu.make_async_remote_copy(
+        src_ref=src, dst_ref=dst, send_sem=send, recv_sem=recv, device_id=(row, col), device_id_type=MESH
+    )
+
+
+def greet(peers):
+    barrier = pltpu.get_barrier_semaphore()
+    for peer in peers:
+        pl.semaphore_signal(barrier, inc=1, device_id=peer, device_id_type=MESH)
+    pl.semaphore_wait(barrier, len(peers))
+
+
+def prepare(upd, slots, diag, lh, ll, th, tl, piece, table, inv, counts):
+    row, col = lax.axis_index("row"), lax.axis_index("col")
+    for i in range(64):
+        table[i] = 0
+    for i in range(16):
+        counts[i] = 0
+
+    def visit(u, carry):
+        slot = slots[upd[u]]
+        owner = slot // 12
+        seen = counts[owner]
+        counts[owner] = seen + 1
+
+        @pl.when(seen >= 6)
+        def _():
+            table[OVER] = 1
+
+        @pl.when((owner == row) & (seen < 6))
+        def _():
+            table[ROWS + seen] = slot - 12 * row
+            table[SLOT + u // 6] = seen
+
+        return carry
+
+    lax.fori_loop(0, UTILES, visit, 0)
+    for k in range(12):
+        table[COLS + k] = upd[12 * col + k] - 24 * col
+    for i in range(6):
+        table[FROM + i] = slots[upd[6 * row + i]] // 12
+
+    inv[...] = jnp.zeros_like(inv)
+    i = lax.broadcasted_iota(jnp.int32, (256, 256), 0)
+    j = lax.broadcasted_iota(jnp.int32, (256, 256), 1)
+    for b in range(4):
+        s = pl.ds(256 * b, 256)
+        inv[s, s] = jnp.where(i == j, 1.0 / diag[s, s], 0.0)
+
+    def level(n, carry):
+        bi, bj = lax.shift_right_logical(i, n), lax.shift_right_logical(j, n)
+        mask = (bi == bj + 1) & ((bi & 1) == 1)
+        for b in range(4):
+            s = pl.ds(256 * b, 256)
+            x = inv[s, s]
+            inv[s, s] = x - exact(x, exact(jnp.where(mask, diag[s, s], 0.0), x))
+        return carry
+
+    lax.fori_loop(0, 8, level, 0)
+    for size in (256, 512):
+        for b in range(512 // size):
+            top, low = pl.ds(2 * size * b, size), pl.ds(2 * size * b + size, size)
+            inv[low, top] = -exact(inv[low, low], exact(diag[low, top], inv[top, top]))
+
+    def out(m, carry):
+        s = pl.ds(pl.multiple_of(m * 128, 128), 128)
+        x = inv[s, :]
+        lh[s, :], ll[s, :] = split(x)
+        th[:, s], tl[:, s] = split(x.T)
+        return carry
+
+    lax.fori_loop(0, 8, out, 0)
+    piece[...] = inv[pl.ds(pl.multiple_of(row * 64, 64), 64), pl.ds(pl.multiple_of(col * 128, 128), 128)]
+
+
+ITEMS = (
+    (0, 0), (0, -1), (0, 1), (-1, 0), (1, 0), (0, 2), (-1, -1), (1, -1),
+    (-1, 1), (1, 1), (2, 0), (-1, 2), (1, 2), (2, -1), (2, 1), (2, 2),
+)
+
+
+def front(
+    table, anc, lb, lh, ll, cov_o, bro,
+    ancv, bg, sh, sl, bh, bl, pa, pb, ph, pq, w, qr, qs, d2r, d1r, brx,
+    anc_sem, gs, gr, xs, ps, sr, es, er, rs, rr, out_sem,
+):
+    row, col = lax.axis_index("row"), lax.axis_index("col")
+    y, z, x, core = row // 4, row % 4, col // 2, col % 2
+    other = 2 * x + 1 - core
+
+    def at(dy, dz):
+        return 4 * lax.rem(y + dy + 4, 4) + lax.rem(z + dz + 4, 4)
+
+    def along(dx):
+        return 2 * lax.rem(x + dx + 4, 4) + core
+
+    loads = [
+        pltpu.make_async_copy(anc.at[:, :, pl.ds(128 * t, 128)], ancv.at[t], anc_sem.at[t])
+        for t in range(24)
+    ]
+    for load in loads:
+        load.start()
+    lane = lax.broadcasted_iota(jnp.int32, (128, 128), 1)
+    for h in range(2):
+        for m in range(3):
+            low = lb[pl.ds(768 * h + 128 * m, 128), :]
+            high = lb[pl.ds(768 * h + 384 + 128 * m, 128), :]
+            bg[row, pl.ds(384 * h + 128 * m, 128), :] = jnp.concatenate([low, high], axis=1)
+    greet(
+        [(at(0, 1), col), (at(0, -1), col), (at(1, 0), col), (at(-1, 0), col)]
+        + [(row, along(1)), (row, along(-1)), (row, other)]
+    )
+
+    def rel(h, a, b):
+        return at(a, b) if h == 0 else at(b, a)
+
+    ids = {}
+    sends = []
+
+    def gather(name, h, src, rows, step, recv_src):
+        k = ids.setdefault((h, name), len(ids))
+        part = pl.ds(384 * h + rows[0], rows[1])
+        view = bg.at[rel(h, *src), part]
+        copy = remote(view, view, gs.at[k], gr.at[k], rel(h, *step), col)
+        copy.start()
+        mine = bg.at[rel(h, *recv_src), part]
+        got = remote(mine, mine, gs.at[k], gr.at[k], rel(h, *step), col)
+        sends.append(copy)
+        return got
+
+    FULL, LOW, HIGH = (0, 384), (0, 192), (192, 192)
+    arr = {}
+
+    def first_phase(h):
+        arr[h, 0, -1] = [gather("f+", h, (0, 0), FULL, (0, 1), (0, -1))]
+        arr[h, 0, 1] = [gather("f-", h, (0, 0), FULL, (0, -1), (0, 1))]
+
+    def first_forward(h):
+        arr[h, 0, 2] = [
+            gather("ff+", h, (0, -1), LOW, (0, 1), (0, -2)),
+            gather("ff-", h, (0, 1), HIGH, (0, -1), (0, 2)),
+        ]
+
+    def second_phase(h, q):
+        arr[h, -1, q] = [gather(("s+", q), h, (0, q), FULL, (1, 0), (-1, q))]
+        arr[h, 1, q] = [gather(("s-", q), h, (0, q), FULL, (-1, 0), (1, q))]
+
+    def second_forward(h, q):
+        arr[h, 2, q] = [
+            gather(("sf+", q), h, (-1, q), LOW, (1, 0), (-2, q)),
+            gather(("sf-", q), h, (1, q), HIGH, (-1, 0), (2, q)),
+        ]
+
+    def wait(h, a, b):
+        for got in arr[h, a, b]:
+            got.wait_recv()
+
+    parity = row % 2
+    root_x, root_core = row // 4, (row // 2) % 2
+    dist = lax.rem(x - root_x + 4, 4)
+    ring = core == root_core
+    S0, S1 = pl.ds(0, 192), pl.ds(192, 192)
+
+    def piece_of(i):
+        a, b = ITEMS[i]
+        index = jnp.where(parity == 0, at(a, b), at(b, a))
+        return index
+
+    def spread_copies(i):
+        def make(part, k, device):
+            view = brx.at[i, part]
+            return remote(view, view, xs.at[i, k], sr.at[i, k], row, device)
+
+        def partner(part, k):
+            view = brx.at[i, part]
+            return remote(view, view, ps.at[i, k], sr.at[i, k], row, other)
+
+        return make(S0, 0, along(1)), make(S1, 1, along(-1)), partner(S0, 0), partner(S1, 1)
+
+    def spread_root(i):
+        @pl.when(ring & (dist == 0))
+        def _():
+            brx[i] = bg[piece_of(i), pl.ds(pl.multiple_of(384 * parity, 384), 384), :]
+            for copy in spread_copies(i):
+                copy.start()
+
+    def spread_hop(i, hop):
+        up, down, pup, pdown = spread_copies(i)
+
+        @pl.when(ring & (dist == hop))
+        def _():
+            up.wait_recv()
+            if hop < 3:
+                up.start()
+            pup.start()
+
+        @pl.when(ring & (dist == 4 - hop))
+        def _():
+            down.wait_recv()
+            if hop < 3:
+                down.start()
+            pdown.start()
+
+    def spread_end(i):
+        up, down, pup, pdown = spread_copies(i)
+
+        @pl.when(ring)
+        def _():
+            pup.wait_send()
+            pdown.wait_send()
+
+            @pl.when(dist != 3)
+            def _():
+                up.wait_send()
+
+            @pl.when(dist != 1)
+            def _():
+                down.wait_send()
+
+        @pl.when(jnp.logical_not(ring))
+        def _():
+            pup.wait_recv()
+            pdown.wait_recv()
+
+    def spread_step(i):
+        if i < 16:
+            spread_root(i)
+        for hop in (1, 2, 3):
+            if 0 <= i - hop < 16:
+                spread_hop(i - hop, hop)
+
+    def product(h, a):
+        lead = lax.rem((y if h == 0 else z) + a + 4, 4)
+        out = pa if h == 0 else pb
+        for half in range(3):
+            rows = pl.ds(384 * h + 128 * half, 128)
+            low, high = pl.ds(128 * half, 128), pl.ds(384 + 128 * half, 128)
+            for pair in range(2):
+                if h == 0:
+                    p0, p1 = bg[4 * lead + 2 * pair, rows, :], bg[4 * lead + 2 * pair + 1, rows, :]
+                else:
+                    p0, p1 = bg[4 * (2 * pair) + lead, rows, :], bg[4 * (2 * pair + 1) + lead, rows, :]
+                cols = pl.ds(128 * pair, 128)
+                bh[low, cols], bl[low, cols] = split(jnp.where(lane < 64, p0, pltpu.roll(p1, 64, 1)))
+                bh[high, cols], bl[high, cols] = split(jnp.where(lane < 64, pltpu.roll(p0, 64, 1), p1))
+
+        def body(m, carry):
+            r = pl.ds(pl.multiple_of(m * 256, 256), 256)
+            k = pl.ds(768 * h, 768)
+            out[lead, r, :] = dot3(sh[r, k], sl[r, k], bh[...], bl[...])
+            return carry
+
+        lax.fori_loop(0, 3, body, 0)
+
+    def extract(j, carry):
+        dst = pl.ds(pl.multiple_of(j * 128, 128), 128)
+        for k in range(12):
+            tile = ancv[table[COLS + k], table[ROWS + j]]
+            c = pl.ds(128 * k, 128)
+            sh[dst, c], sl[dst, c] = split(tile)
+        return carry
+
+    both = (0, 1)
+    for h in both:
+        first_phase(h)
+    for h in both:
+        second_phase(h, 0)
+    spread_step(0)
+    for q in (-1, 1):
+        for h in both:
+            wait(h, 0, q)
+        if q == 1:
+            for h in both:
+                first_forward(h)
+        for h in both:
+            second_phase(h, q)
+    spread_step(1)
+    spread_step(2)
+    for h in both:
+        wait(h, -1, 0)
+        wait(h, 1, 0)
+        second_forward(h, 0)
+    spread_step(3)
+    spread_step(4)
+    for load in loads:
+        load.wait()
+    lax.fori_loop(0, 6, extract, 0)
+    for h in both:
+        wait(h, 0, 2)
+        second_phase(h, 2)
+    spread_step(5)
+    product(0, 0)
+    for q, i in ((-1, 6), (1, 8)):
+        for h in both:
+            wait(h, -1, q)
+            wait(h, 1, q)
+            second_forward(h, q)
+        spread_step(i)
+        spread_step(i + 1)
+        if q == -1:
+            product(1, 0)
+    for h in both:
+        wait(h, 2, 0)
+    spread_step(10)
+    for h in both:
+        wait(h, -1, 2)
+        wait(h, 1, 2)
+        second_forward(h, 2)
+    spread_step(11)
+    spread_step(12)
+    product(0, -1)
+    product(1, -1)
+    for h in both:
+        wait(h, 2, -1)
+        wait(h, 2, 1)
+    spread_step(13)
+    spread_step(14)
+    product(0, 1)
+    product(1, 1)
+    for h in both:
+        wait(h, 2, 2)
+    spread_step(15)
+    product(0, 2)
+    product(1, 2)
+    spread_step(16)
+
+    def combine(m, carry):
+        r = pl.ds(pl.multiple_of(m * 128, 128), 128)
+        for yy in range(4):
+            for pair in range(2):
+                p0 = pb[2 * pair, r, pl.ds(128 * (yy // 2), 128)]
+                p1 = pb[2 * pair + 1, r, pl.ds(128 * (yy // 2), 128)]
+                if yy % 2 == 0:
+                    mixed = jnp.where(lane < 64, p0, pltpu.roll(p1, 64, 1))
+                else:
+                    mixed = jnp.where(lane < 64, pltpu.roll(p0, 64, 1), p1)
+                c = pl.ds(256 * yy + 128 * pair, 128)
+                ph[r, c], pq[r, c] = split(pa[yy, r, pl.ds(128 * pair, 128)] + mixed)
+        return carry
+
+    lax.fori_loop(0, 6, combine, 0)
+    spread_step(17)
+
+    TOP, LOWER = pl.ds(0, 384), pl.ds(384, 384)
+    swaps = []
+
+    def columns(k, dx):
+        c = pl.ds(pl.multiple_of(256 * lax.rem(x + dx + 4, 4), 256), 256)
+
+        def body(m, carry):
+            r = pl.ds(pl.multiple_of(m * 256, 256), 256)
+            acc = dot3(ph[r, :], pq[r, :], lh[:, c], ll[:, c])
+            w[0, k, r, :] = acc[:, :128]
+            w[1, k, r, :] = acc[:, 128:]
+            return carry
+
+        lax.fori_loop(0, 3, body, 0)
+        swap = remote(w.at[1 - core, k], qr.at[k], es.at[k], er.at[k], row, other)
+        swap.start()
+        swaps.append(swap)
+
+    def merged(k):
+        swaps[k].wait_recv()
+        qs[k] = w[core, k] + qr[k]
+
+    columns(0, 2)
+    columns(1, 1)
+    merged(0)
+    up2 = remote(qs.at[0, TOP], d2r.at[0], rs.at[0], rr.at[0], row, along(1))
+    down2 = remote(qs.at[0, LOWER], d2r.at[1], rs.at[1], rr.at[1], row, along(-1))
+    up2.start()
+    down2.start()
+    columns(2, -1)
+    merged(1)
+    up_raw = remote(qs.at[1, LOWER], d1r.at[0, LOWER], rs.at[2], rr.at[2], row, along(1))
+    up_raw.start()
+    columns(3, 0)
+    merged(2)
+    down_raw = remote(qs.at[2, TOP], d1r.at[1, TOP], rs.at[3], rr.at[3], row, along(-1))
+    down_raw.start()
+    merged(3)
+    spread_step(18)
+    up2.wait_recv()
+    qs[1, TOP] += d2r[0]
+    up_sum = remote(qs.at[1, TOP], d1r.at[0, TOP], rs.at[4], rr.at[4], row, along(1))
+    up_sum.start()
+    down2.wait_recv()
+    qs[2, LOWER] += d2r[1]
+    down_sum = remote(qs.at[2, LOWER], d1r.at[1, LOWER], rs.at[5], rr.at[5], row, along(-1))
+    down_sum.start()
+    for i in range(16):
+        spread_end(i)
+    store = pltpu.make_async_copy(brx, bro, out_sem)
+    store.start()
+    for copy in sends:
+        copy.wait_send()
+    up_raw.wait_recv()
+    down_raw.wait_recv()
+    up_sum.wait_recv()
+    down_sum.wait_recv()
+    for t in range(6):
+        r = pl.ds(128 * t, 128)
+        cov_o[t] = -(qs[3, r] + d1r[0, r] + d1r[1, r])
+    for copy in swaps + [up2, down2, up_raw, down_raw, up_sum, down_sum]:
+        copy.wait_send()
+    store.wait()
+
+
+def back(
+    table, cov_o, bro, th, tl, piece, cov, diag,
+    slots, inc, brh, brl, wp, ws, wr, wall, ch, cl, as_, ar, bs, br, cs, cr,
+):
+    row, col = lax.axis_index("row"), lax.axis_index("col")
+    y, z = row // 4, row % 4
+
+    def at(dy, dz):
+        return 4 * lax.rem(y + dy + 4, 4) + lax.rem(z + dz + 4, 4)
+
+    peers = [lax.rem(row + d, 16) for d in range(1, 16)]
+    origins = [lax.rem(row + 16 - d, 16) for d in range(1, 16)]
+    greet([(peer, col) for peer in peers])
+    for t in range(16):
+        slots[t] = cov_o[table[SLOT + t]]
+    tiles = []
+    for k, peer in enumerate(peers):
+        copy = remote(slots.at[peer], inc.at[row], as_.at[k], ar.at[k], peer, col)
+        copy.start()
+        tiles.append(copy)
+    inc[row] = slots[row]
+    parity = row % 2
+    for i, (a, b) in enumerate(ITEMS):
+        index = jnp.where(parity == 0, at(a, b), at(b, a))
+        t = bro[i].T
+        dst = pl.ds(pl.multiple_of(index * 64, 64), 64)
+        brh[dst, pl.ds(0, 384)], brl[dst, pl.ds(0, 384)] = split(t[:64])
+        brh[dst, pl.ds(384, 384)], brl[dst, pl.ds(384, 384)] = split(t[64:])
+    for k, copy in enumerate(tiles):
+        mine = inc.at[origins[k]]
+        remote(mine, mine, as_.at[k], ar.at[k], peers[k], col).wait_recv()
+    for i in range(6):
+        tile = inc[table[FROM + i]]
+        r = pl.ds(128 * i, 128)
+        cov[r, :] = tile
+        ch[r, :], cl[r, :] = split(tile)
+
+    def cross(m, carry):
+        r = pl.ds(pl.multiple_of(m * 256, 256), 256)
+        wp[r, :] = dot3(brh[r, :], brl[r, :], ch[pl.ds(0, 768), :], cl[pl.ds(0, 768), :])
+        return carry
+
+    lax.fori_loop(0, 4, cross, 0)
+    parts = []
+    for k, peer in enumerate(peers):
+        src = wp.at[pl.ds(pl.multiple_of(peer * 64, 64), 64)]
+        copy = remote(src, wr.at[row], bs.at[k], br.at[k], peer, col)
+        copy.start()
+        parts.append(copy)
+    total = piece[...] - wp[pl.ds(pl.multiple_of(row * 64, 64), 64), :]
+    for k in range(15):
+        mine = wr.at[origins[k]]
+        remote(mine, mine, bs.at[k], br.at[k], peers[k], col).wait_recv()
+        total -= wr[origins[k]]
+    wall[row] = total
+    ends = []
+    for k, peer in enumerate(peers):
+        copy = remote(wall.at[row], wall.at[row], cs.at[k], cr.at[k], peer, col)
+        copy.start()
+        ends.append(copy)
+    for k in range(15):
+        mine = wall.at[origins[k]]
+        remote(mine, mine, cs.at[k], cr.at[k], peers[k], col).wait_recv()
+    vh, vl = split(wall[...].reshape(1024, 128))
+    ch[...] = vh
+    cl[...] = vl
+
+    def last(m, carry):
+        r = pl.ds(pl.multiple_of(m * 256, 256), 256)
+        diag[r, :] = dot3(th[r, :], tl[r, :], ch[...], cl[...])
+        return carry
+
+    lax.fori_loop(0, 4, last, 0)
+    for copy in tiles + parts + ends:
+        copy.wait_send()
+
+
+def shape(dims, dtype=F32):
+    return jax.ShapeDtypeStruct(dims, dtype)
+
+
+def shards(ancestor_inv, update_tiles, tile_slot, lower_below, diag_factor):
+    lh, ll, th, tl, piece, table = pl.pallas_call(
+        prepare,
+        out_shape=[shape((JW, JW), BF16)] * 4 + [shape((64, 128)), shape((64,), jnp.int32)],
+        in_specs=[SMEM, SMEM, VMEM],
+        out_specs=[VMEM] * 5 + [SMEM],
+        scratch_shapes=[pltpu.VMEM((JW, JW), F32), pltpu.SMEM((16,), jnp.int32)],
+        compiler_params=pltpu.CompilerParams(vmem_limit_bytes=LIMIT),
+        name="prepare",
+    )(update_tiles, tile_slot, diag_factor)
+
+    def fast(ancestor_inv, update_tiles, tile_slot, lower_below, diag_factor):
+        vm = pltpu.VMEM
+        dma = pltpu.SemaphoreType.DMA
+        cov_o, bro = pl.pallas_call(
+            front,
+            out_shape=[shape((6, 128, 128)), shape((16, 384, 128))],
+            in_specs=[SMEM, ANY, VMEM, VMEM, VMEM],
+            out_specs=[VMEM, ANY],
+            scratch_shapes=[
+                vm((24, 12, 128, 128), F32), vm((16, 768, 128), F32), vm((768, 1536), BF16), vm((768, 1536), BF16),
+                vm((768, 256), BF16), vm((768, 256), BF16), vm((4, 768, 256), F32), vm((4, 768, 256), F32),
+                vm((768, 1024), BF16), vm((768, 1024), BF16), vm((2, 4, 768, 128), F32), vm((4, 768, 128), F32),
+                vm((4, 768, 128), F32), vm((2, 384, 128), F32), vm((2, 768, 128), F32), vm((16, 384, 128), F32),
+                dma((24,)), dma((40,)), dma((40,)), dma((16, 2)), dma((16, 2)), dma((16, 2)),
+                dma((4,)), dma((4,)), dma((6,)), dma((6,)), dma(()),
+            ],
+            compiler_params=pltpu.CompilerParams(vmem_limit_bytes=LIMIT, collective_id=0, has_side_effects=True),
+            name="front",
+        )(table, ancestor_inv.reshape(12, 128, 3072), lower_below, lh, ll)
+        return pl.pallas_call(
+            back,
+            out_shape=[shape((768, 128)), shape((1024, 128))],
+            in_specs=[SMEM] + [VMEM] * 5,
+            out_specs=[VMEM, VMEM],
+            scratch_shapes=[
+                vm((16, 128, 128), F32), vm((16, 128, 128), F32), vm((1024, 768), BF16), vm((1024, 768), BF16),
+                vm((1024, 128), F32), vm((64, 128), F32), vm((16, 64, 128), F32), vm((16, 64, 128), F32),
+                vm((1024, 128), BF16), vm((1024, 128), BF16),
+            ] + [dma((15,))] * 6,
+            compiler_params=pltpu.CompilerParams(vmem_limit_bytes=LIMIT, collective_id=1, has_side_effects=True),
+            name="back",
+        )(table, cov_o, bro, th, tl, piece)
+
+    return lax.cond(
+        table[OVER] == 0, fast, general, ancestor_inv, update_tiles, tile_slot, lower_below, diag_factor
+    )
+
+
 def solution(mesh):
     in_specs = (P("row", "col"), P(), P(), P("col", "row"), P())
     out_specs = (P("row", "col"), P(None, "col"))

time: 589 us -> 187 us (0.32); the launches traced: 580 us -> 185 us
  waiting for transfers between devices: 242 us -> 0 us
  Pallas kernels: 0 us -> 165 us
  local copies, waits for them, and re-layouts: 123 us -> 4.28 us
  other arithmetic: 113 us -> 0 us
  matrix products: 77.1 us -> 0 us
  starting transfers between devices: 9.25 us -> 0 us
    pallas_call x0 -> x3, Pallas kernels: none -> 165 us  [the longest x1 84.5 us: fast(): pl.pallas_call(front, out_shape=[shape((6, 128, 128)), shape((16, 384, 12...]
    psum x2 -> x0, waiting for transfers between devices: 158 us -> none  [the longest x1 87.9 us: shards(): cross = lax.psum(jnp.dot(front_scaled.T, cov_below, precision=exact), 'row')]
    another operation x3 -> x0, other arithmetic: 83.3 us -> none  [solve_right(): jax.scipy.linalg.solve_triangular(factor, rows.T, lower=True, trans=1)]
    all_to_all x1 -> x0, waiting for transfers between devices: 68.1 us -> none  [shards(): lax.all_to_all(outgoing, 'row', split_axis=0, concat_axis=0, tiled=True)]
    gather x8 -> x0, local copies, waits for them, and re-layouts: 55.5 us -> none  [the longest x3 35.9 us: shards(): jnp.take(tiled, col_tiles, axis=1)]
    another operation x45 -> x0, matrix products: 53.5 us -> none  [the longest x15 29.5 us: solve_right(): jax.scipy.linalg.solve_triangular(factor, rows.T, lower=True, trans=1)]
    unnamed x47 -> x2, local copies, waits for them, and re-layouts: 25.3 us -> 1.54 us
    dot_general x2 -> x0, matrix products: 23.7 us -> none  [the longest x1 18.4 us: shards(): row_terms = jnp.dot(front_tiles, scaled, precision=exact)]
  transfers between devices with their start and end apart: 5 -> 0, of which waited for: 4 -> 0; matrix products, arithmetic and copies ran while one was open for 48% -> 0% of each run, Pallas kernels for 0% -> 0%
where the time goes in v1:
time: 187 us; the launch traced here: 185 us
  Pallas kernels  165 us (88%)
  between operations  14.7 us (8%)
  local copies, waits for them, and re-layouts  4.28 us (2%)
    pallas_call x1, Pallas kernels, fast(): pl.pallas_call(front, out_shape=[shape((6, 128, 128)), shape((16, 384, 12...  84.5 us
    pallas_call x1, Pallas kernels, fast(): pl.pallas_call(back, out_shape=[shape((768, 128)), shape((1024, 128))], i...  47.4 us
    pallas_call x1, Pallas kernels, shards(): pl.pallas_call(prepare, out_shape=[shape((JW, JW), BF16)] * 4 + [shape((6...  33.4 us

profile of v1, /device:TPU:6, one launch (start us, length us, event | category | flops | bytes accessed | tf_op | source)
XLA Modules:
  0.0 184.8 jit_solution(15203084920812646815)
XLA Ops:
  7.2 33.4 %prepare.1 = (bf16[1024,1024]{1,0:T(8,128)(2,1)S(1)}, bf16[1024,1024]{1,0:T(8,128)(2,1)}, bf16[1024,1024]{1,0:T(8,128)(2,1)}, bf16[1024,1024]{1,0:T(8,128)(2,1)}, f32[64,128]{1,0:T(8,128)S(1)}, /*index=5*/s32[64]{0:T(128)S(1)}) custom-call(s32[96]{0:T(128)} %upd.1, s32[192]{0:T(256)} %slots.1, f32[1024,1024]{1,0:T(8,128)} %diag.1), custom_call_target="tpu_custom_call" | custom-call | tf_op jit(solution)/shard_map/prepare/pallas_call | solution.py:598
  40.6 0.6 slice.210
  41.8 134.6 %conditional.1 = ((f32[768,128]{1,0:T(8,128)S(1)}, f32[1024,128]{1,0:T(8,128)S(1)})) conditional(s32[]{:T(128)} %bitcast.18, (s32[96]{0:T(128)}, s32[192]{0:T(256)}, f32[1536,3072]{1,0:T(8,128)}, f32[1024,1024]{1,0:T(8,128)}, f32[1536,64]{0,1:T(8,128)}) %tuple.15, (f32[1536,3072]{1,0:T(8,128)}, s32[64]{0:T(128)S(1)}, f32[1536,64]{0,1:T(8,128)}, ...), branch_computations={%region_0.8_spmd, %region_7.9_spmd} | conditional | flops 28407451648 | bytes 473358720 | solution.py:641
  42.1 2.2 %copy.21.lb = f32[1536,64]{1,0:T(8,128)} copy(f32[1536,64]{0,1:T(8,128)} %get-tuple-element.113) | data formatting | bytes 786432 | tf_op jit(solution)/shard_map
  44.2 84.5 %front.1 = (f32[6,128,128]{2,1,0:T(8,128)}, f32[16,384,128]{2,1,0:T(8,128)}) custom-call(s32[64]{0:T(128)S(1)} %get-tuple-element.32.table, f32[12,128,3072]{2,1,0:T(8,128)} %bitcast.131, f32[1536,64]{1,0:T(8,128)} %copy.21.lb, bf16[1024,1024]{1,0:T(8,128)(2,1)S(1)} %get-tuple-element.35.lh, bf16[1024,1024]{1,0:T(8,128)(2,1)} %get-tuple-element.36.ll), custom_call_target="tpu_custom_call" | custom-call | tf_op jit(solution)/shard_map/cond/branch_1_fun/front/pallas_call | solution.py:611
  128.8 47.4 %back.1 = (f32[768,128]{1,0:T(8,128)S(1)}, f32[1024,128]{1,0:T(8,128)S(1)}) custom-call(s32[64]{0:T(128)S(1)} %get-tuple-element.32.table, f32[6,128,128]{2,1,0:T(8,128)} %get-tuple-element.37.cov_o, f32[16,384,128]{2,1,0:T(8,128)} %get-tuple-element.38.bro, bf16[1024,1024]{1,0:T(8,128)(2,1)} %get-tuple-element.39.th, ...), custom_call_target="tpu_custom_call" | custom-call | tf_op jit(solution)/shard_map/cond/branch_1_fun/back/pallas_call | solution.py:627
  176.4 0.7 copy.97
  177.2 0.8 copy.98

commit v2 on v0

--- a/solution.py
+++ b/solution.py
@@ -1,12 +1,22 @@
 import jax
 import jax.numpy as jnp
 from jax import lax
+from jax.experimental import pallas as pl
+from jax.experimental.pallas import tpu as pltpu
 from jax.sharding import PartitionSpec as P
 
 TILE = 128
 ATILES = 192
 UTILES = 96
 JW = 1024
+MESH = pl.DeviceIdType.MESH
+F32, BF16 = jnp.float32, jnp.bfloat16
+VMEM = pl.BlockSpec(memory_space=pltpu.VMEM)
+SMEM = pl.BlockSpec(memory_space=pltpu.SMEM)
+ANY = pl.BlockSpec(memory_space=pl.ANY)
+LIMIT = 60 * 1024 * 1024
+ROWS, COLS, SLOT, FROM, OVER = 0, 8, 20, 36, 42
+FULL, LOW, HIGH = (0, 32), (0, 16), (16, 16)
 
 
 def spread(value, axis, root):
@@ -18,7 +28,7 @@
     return jax.scipy.linalg.solve_triangular(factor, rows.T, lower=True, trans=1).T
 
 
-def shards(ancestor_inv, update_tiles, tile_slot, lower_below, diag_factor):
+def general(ancestor_inv, update_tiles, tile_slot, lower_below, diag_factor):
     rows_count = lax.axis_size("row")
     cols_count = lax.axis_size("col")
     this_row = lax.axis_index("row")
@@ -80,6 +90,578 @@
     return (cov_below, cov_diag)
 
 
+def split(value):
+    high = value.astype(BF16)
+    return high, (value - high.astype(F32)).astype(BF16)
+
+
+def dot3(ah, al, bh, bl):
+    out = jnp.dot(ah, bh, preferred_element_type=F32)
+    out += jnp.dot(ah, bl, preferred_element_type=F32)
+    return out + jnp.dot(al, bh, preferred_element_type=F32)
+
+
+def remote(src, dst, send, recv, row, col):
+    return pltpu.make_async_remote_copy(
+        src_ref=src, dst_ref=dst, send_sem=send, recv_sem=recv, device_id=(row, col), device_id_type=MESH
+    )
+
+
+def greet(peers):
+    barrier = pltpu.get_barrier_semaphore()
+    for peer in peers:
+        pl.semaphore_signal(barrier, inc=1, device_id=peer, device_id_type=MESH)
+    pl.semaphore_wait(barrier, len(peers))
+
+
+def tables(upd, slots, table, counts):
+    row, col = lax.axis_index("row"), lax.axis_index("col")
+    for i in range(64):
+        table[i] = 0
+    for i in range(16):
+        counts[i] = 0
+
+    def visit(u, carry):
+        slot = slots[upd[u]]
+        owner = slot // 12
+        seen = counts[owner]
+        counts[owner] = seen + 1
+
+        @pl.when(seen >= 6)
+        def _():
+            table[OVER] = 1
+
+        @pl.when((owner == row) & (seen < 6))
+        def _():
+            table[ROWS + seen] = slot - 12 * row
+            table[SLOT + u // 6] = seen
+
+        return carry
+
+    lax.fori_loop(0, UTILES, visit, 0)
+    for k in range(12):
+        table[COLS + k] = upd[12 * col + k] - 24 * col
+    for i in range(6):
+        table[FROM + i] = slots[upd[6 * row + i]] // 12
+
+
+ITEMS = (
+    (0, 0), (0, -1), (0, 1), (-1, 0), (1, 0), (0, 2), (2, 0), (-1, -1),
+    (1, -1), (-1, 1), (1, 1), (-1, 2), (1, 2), (2, -1), (2, 1), (2, 2),
+)
+
+
+def work(
+    table, anc, lbt, diag, cov, cov_diag,
+    ancv, bg, sh, sl, bh, bl, ph, pq, qr, d2r, d1r, brx, dg, inv, lh, ll,
+    co, slots, inc, wp, wr, wall, ch, cl,
+    anc_sem, own_sem, dg_sem, gs, gr, xs, ps, sr, es, er, rs, rr, is_, ir, as_, ar, bs, br, cs, cr,
+):
+    row, col = lax.axis_index("row"), lax.axis_index("col")
+    y, z, x, core = row // 4, row % 4, col // 2, col % 2
+    other = 2 * x + 1 - core
+
+    def at(dy, dz):
+        return 4 * lax.rem(y + dy + 4, 4) + lax.rem(z + dz + 4, 4)
+
+    def along(dx):
+        return 2 * lax.rem(x + dx + 4, 4) + core
+
+    own = pltpu.make_async_copy(lbt, bg.at[row], own_sem)
+    own.start()
+    dg_load = pltpu.make_async_copy(diag, dg, dg_sem)
+    dg_load.start()
+    loads = [
+        pltpu.make_async_copy(anc.at[:, :, pl.ds(128 * t, 128)], ancv.at[t], anc_sem.at[t])
+        for t in range(24)
+    ]
+    for load in loads:
+        load.start()
+    peers = [lax.rem(row + d, 16) for d in range(1, 16)]
+    origins = [lax.rem(row + 16 - d, 16) for d in range(1, 16)]
+    greet([(peer, col) for peer in peers] + [(row, along(1)), (row, along(-1)), (row, other)])
+    own.wait()
+
+    def rel(h, a, b):
+        return at(a, b) if h == 0 else at(b, a)
+
+    ids = {}
+    sends = []
+
+    def gather(name, h, src, rows, step, recv_src):
+        k = ids.setdefault((h, name), len(ids))
+        part = pl.ds(32 * h + rows[0], rows[1])
+        view = bg.at[rel(h, *src), part]
+        copy = remote(view, view, gs.at[k], gr.at[k], rel(h, *step), col)
+        copy.start()
+        mine = bg.at[rel(h, *recv_src), part]
+        got = remote(mine, mine, gs.at[k], gr.at[k], rel(h, *step), col)
+        sends.append(copy)
+        return got
+
+    arr = {}
+
+    def first_phase(h):
+        arr[h, 0, -1] = [gather("f+", h, (0, 0), FULL, (0, 1), (0, -1))]
+        arr[h, 0, 1] = [gather("f-", h, (0, 0), FULL, (0, -1), (0, 1))]
+
+    def first_forward(h):
+        arr[h, 0, 2] = [
+            gather("ff+", h, (0, -1), LOW, (0, 1), (0, -2)),
+            gather("ff-", h, (0, 1), HIGH, (0, -1), (0, 2)),
+        ]
+
+    def second_phase(h, q):
+        arr[h, -1, q] = [gather(("s+", q), h, (0, q), FULL, (1, 0), (-1, q))]
+        arr[h, 1, q] = [gather(("s-", q), h, (0, q), FULL, (-1, 0), (1, q))]
+
+    def second_forward(h, q):
+        arr[h, 2, q] = [
+            gather(("sf+", q), h, (-1, q), LOW, (1, 0), (-2, q)),
+            gather(("sf-", q), h, (1, q), HIGH, (-1, 0), (2, q)),
+        ]
+
+    def wait(h, a, b):
+        for got in arr[h, a, b]:
+            got.wait_recv()
+
+    parity = row % 2
+    root_x, root_core = row // 4, (row // 2) % 2
+    dist = lax.rem(x - root_x + 4, 4)
+    ring = core == root_core
+
+    def spread_copies(i):
+        def make(h, device):
+            view = brx.at[i, pl.ds(32 * h, 32)]
+            return remote(view, view, xs.at[i, h], sr.at[i, h], row, device)
+
+        def partner(h):
+            view = brx.at[i, pl.ds(32 * h, 32)]
+            return remote(view, view, ps.at[i, h], sr.at[i, h], row, other)
+
+        return make(0, along(1)), make(1, along(-1)), partner(0), partner(1)
+
+    def spread_root(i):
+        @pl.when(ring & (dist == 0))
+        def _():
+            lanes = pl.ds(pl.multiple_of(768 * parity, 768), 768)
+            for h in range(2):
+                brx[i, pl.ds(32 * h, 32), :] = bg[rel(h, *ITEMS[i]), pl.ds(32 * h, 32), lanes]
+            for copy in spread_copies(i):
+                copy.start()
+
+    def spread_hop(i, hop):
+        up, down, pup, pdown = spread_copies(i)
+
+        @pl.when(ring & (dist == hop))
+        def _():
+            up.wait_recv()
+            if hop < 3:
+                up.start()
+            pup.start()
+
+        @pl.when(ring & (dist == 4 - hop))
+        def _():
+            down.wait_recv()
+            if hop < 3:
+                down.start()
+            pdown.start()
+
+    def spread_end(i):
+        up, down, pup, pdown = spread_copies(i)
+
+        @pl.when(ring)
+        def _():
+            pup.wait_send()
+            pdown.wait_send()
+
+            @pl.when(dist != 3)
+            def _():
+                up.wait_send()
+
+            @pl.when(dist != 1)
+            def _():
+                down.wait_send()
+
+        @pl.when(jnp.logical_not(ring))
+        def _():
+            pup.wait_recv()
+            pdown.wait_recv()
+
+    def spread_step(i):
+        if i < 16:
+            spread_root(i)
+        for hop in (1, 2, 3):
+            if 0 <= i - hop < 16:
+                spread_hop(i - hop, hop)
+
+    def extract(j, carry):
+        for k in range(12):
+            high, low = split(ancv[table[COLS + k], table[ROWS + j]])
+            c = pl.ds(128 * k, 128)
+            for half in range(2):
+                dst = pl.ds(pl.multiple_of(384 * half + j * 64, 64), 64)
+                sh[dst, c] = high[64 * half : 64 * half + 64]
+                sl[dst, c] = low[64 * half : 64 * half + 64]
+        return carry
+
+    base = pl.multiple_of(512 * core, 512)
+    i256 = lax.broadcasted_iota(jnp.int32, (256, 256), 0)
+    j256 = lax.broadcasted_iota(jnp.int32, (256, 256), 1)
+
+    def sub(b, size):
+        return pl.ds(pl.multiple_of(base + size * b, size), size)
+
+    def inverse_start():
+        dg_load.wait()
+        inv[pl.ds(0, 512), pl.ds(512, 512)] = jnp.zeros((512, 512), F32)
+        inv[sub(0, 256), sub(1, 256)] = jnp.zeros((256, 256), F32)
+        for b in range(2):
+            s = sub(b, 256)
+            inv[s, s] = jnp.where(i256 == j256, 1.0 / dg[s, s], 0.0)
+
+    def inverse_levels(first, last):
+        def level(n, carry):
+            bi, bj = lax.shift_right_logical(i256, n), lax.shift_right_logical(j256, n)
+            mask = (bi == bj + 1) & ((bi & 1) == 1)
+            for b in range(2):
+                s = sub(b, 256)
+                value = inv[s, s]
+                part = split(value)
+                inner = dot3(*split(jnp.where(mask, dg[s, s], 0.0)), *part)
+                inv[s, s] = value - dot3(*part, *split(inner))
+            return carry
+
+        lax.fori_loop(first, last, level, 0)
+
+    swap_inv = []
+
+    def inverse_512():
+        top, low = sub(0, 256), sub(1, 256)
+        inner = dot3(*split(dg[low, top]), *split(inv[top, top]))
+        inv[low, top] = -dot3(*split(inv[low, low]), *split(inner))
+        block = inv.at[pl.ds(base, 512), pl.ds(base, 512)]
+        copy = remote(block, block, is_, ir, row, other)
+        copy.start()
+        swap_inv.append(copy)
+
+    def inverse_1024():
+        there = pl.ds(pl.multiple_of(512 - base, 512), 512)
+        block = inv.at[there, there]
+        remote(block, block, is_, ir, row, other).wait_recv()
+        top, low = pl.ds(0, 512), pl.ds(512, 512)
+        xh, xl = split(inv[top, top])
+        for m in range(2):
+            r = pl.ds(512 + 256 * m, 256)
+            inner = dot3(*split(dg[r, top]), xh, xl)
+            dg[r, top] = inner
+        ih, il = split(dg[low, top])
+        for m in range(2):
+            r = pl.ds(512 + 256 * m, 256)
+            inv[r, top] = -dot3(*split(inv[r, low]), ih, il)
+
+    def inverse_rows():
+        for i, item in enumerate(ITEMS):
+            for h in range(2):
+                src = pl.ds(pl.multiple_of(64 * rel(h, *item) + 32 * h, 32), 32)
+                dst = pl.ds(64 * i + 32 * h, 32)
+                lh[dst, :], ll[dst, :] = split(inv[src, :])
+
+    def build(g):
+        for p in range(2):
+            for k in range(12):
+                lanes = pl.ds(128 * k, 128)
+                rows = [
+                    bg[rel(h, *ITEMS[4 * g + 2 * p + i]), pl.ds(32 * h, 32), lanes]
+                    for i in range(2)
+                    for h in range(2)
+                ]
+                c = pl.ds(128 * p, 128)
+                bh[lanes, c], bl[lanes, c] = split(jnp.concatenate(rows, axis=0).T)
+
+    def product(g, chunk):
+        r = pl.ds(384 * chunk, 384)
+        c = pl.ds(256 * g, 256)
+        ph[r, c], pq[r, c] = split(dot3(sh[r, :], sl[r, :], bh[...], bl[...]))
+
+    def group(g):
+        build(g)
+        for chunk in range(2):
+            product(g, chunk)
+
+    def block(dx):
+        return pl.ds(pl.multiple_of(256 * lax.rem(x + dx + 4, 4), 256), 256)
+
+    DX = (2, 1, -1, 0)
+    EARLY, LATE = pl.ds(0, 768), pl.ds(768, 256)
+
+    def early_columns(k):
+        c = block(DX[k])
+        for chunk in range(2):
+            r = pl.ds(384 * chunk, 384)
+            acc = dot3(ph[r, EARLY], pq[r, EARLY], lh[EARLY, c], ll[EARLY, c])
+            for half in range(2):
+                ancv[2 * k + half, pl.ds(3 * chunk, 3)] = acc[:, 128 * half : 128 * half + 128].reshape(3, 128, 128)
+
+    both = (0, 1)
+    for h in both:
+        first_phase(h)
+    for h in both:
+        second_phase(h, 0)
+    spread_step(0)
+    inverse_start()
+    inverse_levels(0, 4)
+    for q in (-1, 1):
+        for h in both:
+            wait(h, 0, q)
+        if q == 1:
+            for h in both:
+                first_forward(h)
+        for h in both:
+            second_phase(h, q)
+    spread_step(1)
+    spread_step(2)
+    for load in loads:
+        load.wait()
+    lax.fori_loop(0, 6, extract, 0)
+    for h in both:
+        wait(h, -1, 0)
+        wait(h, 1, 0)
+        second_forward(h, 0)
+    spread_step(3)
+    spread_step(4)
+    inverse_levels(4, 8)
+    for h in both:
+        wait(h, 0, 2)
+        second_phase(h, 2)
+    spread_step(5)
+    inverse_512()
+    for h in both:
+        wait(h, 2, 0)
+    spread_step(6)
+    for q, i in ((-1, 7), (1, 9)):
+        for h in both:
+            wait(h, -1, q)
+            wait(h, 1, q)
+            second_forward(h, q)
+        spread_step(i)
+        spread_step(i + 1)
+        group(0 if q == -1 else 1)
+    inverse_1024()
+    inverse_rows()
+    for h in both:
+        wait(h, -1, 2)
+        wait(h, 1, 2)
+        second_forward(h, 2)
+    spread_step(11)
+    spread_step(12)
+    group(2)
+    for h in both:
+        wait(h, 2, -1)
+        wait(h, 2, 1)
+    spread_step(13)
+    spread_step(14)
+    for k in range(4):
+        early_columns(k)
+    for h in both:
+        wait(h, 2, 2)
+    spread_step(15)
+    build(3)
+
+    UPPER, LOWER = pl.ds(0, 64), pl.ds(64, 64)
+    swaps, moves = {}, {}
+
+    def tiles(chunk):
+        return pl.ds(3 * chunk, 3)
+
+    def columns(chunk, k):
+        r = pl.ds(384 * chunk, 384)
+        c = block(DX[k])
+        acc = dot3(ph[r, LATE], pq[r, LATE], lh[LATE, c], ll[LATE, c])
+        for half in range(2):
+            part = acc[:, 128 * half : 128 * half + 128].reshape(3, 128, 128)
+            ancv[8 + 4 * half + k, tiles(chunk)] = ancv[2 * k + half, tiles(chunk)] + part
+        copy = remote(
+            ancv.at[8 + 4 * (1 - core) + k, tiles(chunk)], qr.at[k, tiles(chunk)],
+            es.at[chunk, k], er.at[chunk, k], row, other,
+        )
+        copy.start()
+        swaps[chunk, k] = copy
+
+    def merged(chunk, k):
+        swaps[chunk, k].wait_recv()
+        ancv[16 + k, tiles(chunk)] = ancv[8 + 4 * core + k, tiles(chunk)] + qr[k, tiles(chunk)]
+
+    def move(chunk, n, k, part, dst, dx):
+        copy = remote(
+            ancv.at[16 + k, tiles(chunk), part], dst, rs.at[chunk, n], rr.at[chunk, n], row, along(dx)
+        )
+        copy.start()
+        moves[chunk, n] = copy
+
+    def far(chunk):
+        move(chunk, 0, 0, UPPER, d2r.at[chunk, 0], 1)
+        move(chunk, 1, 0, LOWER, d2r.at[chunk, 1], -1)
+
+    def near_up(chunk):
+        move(chunk, 2, 1, LOWER, d1r.at[chunk, 0, :, LOWER], 1)
+
+    def near_down(chunk):
+        move(chunk, 3, 2, UPPER, d1r.at[chunk, 1, :, UPPER], -1)
+
+    def passed(chunk):
+        moves[chunk, 0].wait_recv()
+        ancv[17, tiles(chunk), UPPER] += d2r[chunk, 0]
+        move(chunk, 4, 1, UPPER, d1r.at[chunk, 0, :, UPPER], 1)
+        moves[chunk, 1].wait_recv()
+        ancv[18, tiles(chunk), LOWER] += d2r[chunk, 1]
+        move(chunk, 5, 2, LOWER, d1r.at[chunk, 1, :, LOWER], -1)
+
+    tile_copies = {}
+
+    def finish(chunk):
+        for n in (2, 3, 4, 5):
+            moves[chunk, n].wait_recv()
+        for t in range(3):
+            total = -(ancv[19, 3 * chunk + t] + d1r[chunk, 0, t] + d1r[chunk, 1, t])
+            co[chunk, 2 * t] = total[:64]
+            co[chunk, 2 * t + 1] = total[64:]
+        for t in range(16):
+            slots[chunk, t] = co[chunk, table[SLOT + t]]
+        for k, peer in enumerate(peers):
+            copy = remote(slots.at[chunk, peer], inc.at[chunk, row], as_.at[chunk, k], ar.at[chunk, k], peer, col)
+            copy.start()
+            tile_copies[chunk, k] = copy
+        inc[chunk, row] = slots[chunk, row]
+
+    product(3, 0)
+    columns(0, 0)
+    columns(0, 1)
+    merged(0, 0)
+    far(0)
+    columns(0, 2)
+    merged(0, 1)
+    near_up(0)
+    columns(0, 3)
+    merged(0, 2)
+    near_down(0)
+    spread_step(16)
+    product(3, 1)
+    merged(0, 3)
+    columns(1, 0)
+    passed(0)
+    columns(1, 1)
+    merged(1, 0)
+    far(1)
+    columns(1, 2)
+    merged(1, 1)
+    near_up(1)
+    columns(1, 3)
+    merged(1, 2)
+    near_down(1)
+    merged(1, 3)
+    spread_step(17)
+    finish(0)
+    passed(1)
+    spread_step(18)
+    for i in range(16):
+        spread_end(i)
+    for m in range(8):
+        s = pl.ds(128 * m, 128)
+        lh[:, s], ll[:, s] = split(inv[s, :].T)
+    finish(1)
+
+    for chunk in range(2):
+        for k in range(15):
+            mine = inc.at[chunk, origins[k]]
+            remote(mine, mine, as_.at[chunk, k], ar.at[chunk, k], peers[k], col).wait_recv()
+    for i in range(6):
+        for half in range(2):
+            tile = inc[half, table[FROM + i]]
+            r = pl.ds(128 * i + 64 * half, 64)
+            cov[r, :] = tile
+            ch[r, :], cl[r, :] = split(tile)
+    for m in range(4):
+        rows = brx[pl.ds(4 * m, 4)].reshape(256, 768)
+        part = dot3(*split(rows), ch[pl.ds(0, 768), :], cl[pl.ds(0, 768), :])
+        for i in range(4):
+            for h in range(2):
+                dst = pl.ds(pl.multiple_of(64 * rel(h, *ITEMS[4 * m + i]) + 32 * h, 32), 32)
+                wp[dst, :] = part[64 * i + 32 * h : 64 * i + 32 * h + 32]
+    parts = []
+    for k, peer in enumerate(peers):
+        src = wp.at[pl.ds(pl.multiple_of(peer * 64, 64), 64)]
+        copy = remote(src, wr.at[row], bs.at[k], br.at[k], peer, col)
+        copy.start()
+        parts.append(copy)
+    here = pl.ds(pl.multiple_of(row * 64, 64), 64)
+    total = inv[here, pl.ds(pl.multiple_of(col * 128, 128), 128)] - wp[here, :]
+    for k in range(15):
+        mine = wr.at[origins[k]]
+        remote(mine, mine, bs.at[k], br.at[k], peers[k], col).wait_recv()
+        total -= wr[origins[k]]
+    wall[row] = total
+    ends = []
+    for k, peer in enumerate(peers):
+        copy = remote(wall.at[row], wall.at[row], cs.at[k], cr.at[k], peer, col)
+        copy.start()
+        ends.append(copy)
+    for k in range(15):
+        mine = wall.at[origins[k]]
+        remote(mine, mine, cs.at[k], cr.at[k], peers[k], col).wait_recv()
+    ch[...], cl[...] = split(wall[...].reshape(1024, 128))
+    for m in range(4):
+        r = pl.ds(256 * m, 256)
+        cov_diag[r, :] = dot3(lh[r, :], ll[r, :], ch[...], cl[...])
+    for copy in sends + swap_inv + list(swaps.values()) + list(moves.values()) + list(tile_copies.values()):
+        copy.wait_send()
+    for copy in parts + ends:
+        copy.wait_send()
+
+
+def shape(dims, dtype=F32):
+    return jax.ShapeDtypeStruct(dims, dtype)
+
+
+def shards(ancestor_inv, update_tiles, tile_slot, lower_below, diag_factor):
+    table = pl.pallas_call(
+        tables,
+        out_shape=shape((64,), jnp.int32),
+        in_specs=[SMEM, SMEM],
+        out_specs=SMEM,
+        scratch_shapes=[pltpu.SMEM((16,), jnp.int32)],
+        name="tables",
+    )(update_tiles, tile_slot)
+
+    def fast(ancestor_inv, update_tiles, tile_slot, lower_below, diag_factor):
+        vm = pltpu.VMEM
+        dma = pltpu.SemaphoreType.DMA
+        return pl.pallas_call(
+            work,
+            out_shape=[shape((768, 128)), shape((1024, 128))],
+            in_specs=[SMEM, ANY, ANY, ANY],
+            out_specs=[VMEM, VMEM],
+            scratch_shapes=[
+                vm((24, 12, 128, 128), F32), vm((16, 64, 1536), F32), vm((768, 1536), BF16), vm((768, 1536), BF16),
+                vm((1536, 256), BF16), vm((1536, 256), BF16), vm((768, 1024), BF16), vm((768, 1024), BF16),
+                vm((4, 6, 128, 128), F32), vm((2, 2, 3, 64, 128), F32), vm((2, 2, 3, 128, 128), F32),
+                vm((16, 64, 768), F32), vm((1024, 1024), F32), vm((1024, 1024), F32), vm((1024, 1024), BF16),
+                vm((1024, 1024), BF16), vm((2, 6, 64, 128), F32), vm((2, 16, 64, 128), F32), vm((2, 16, 64, 128), F32),
+                vm((1024, 128), F32), vm((16, 64, 128), F32), vm((16, 64, 128), F32), vm((1024, 128), BF16),
+                vm((1024, 128), BF16),
+                dma((24,)), dma(()), dma(()), dma((40,)), dma((40,)), dma((16, 2)), dma((16, 2)), dma((16, 2)),
+                dma((2, 4)), dma((2, 4)), dma((2, 6)), dma((2, 6)), dma(()), dma(()), dma((2, 15)), dma((2, 15)),
+                dma((15,)), dma((15,)), dma((15,)), dma((15,)),
+            ],
+            compiler_params=pltpu.CompilerParams(vmem_limit_bytes=LIMIT, collective_id=0, has_side_effects=True),
+            name="work",
+        )(table, ancestor_inv.reshape(12, 128, 3072), lower_below.T, diag_factor)
+
+    return lax.cond(
+        table[OVER] == 0, fast, general, ancestor_inv, update_tiles, tile_slot, lower_below, diag_factor
+    )
+
+
 def solution(mesh):
     in_specs = (P("row", "col"), P(), P(), P("col", "row"), P())
     out_specs = (P("row", "col"), P(None, "col"))

time: 589 us -> 156 us (0.26); the launches traced: 580 us -> 156 us
  waiting for transfers between devices: 242 us -> 0 us
  Pallas kernels: 0 us -> 131 us
  local copies, waits for them, and re-layouts: 123 us -> 2.12 us
  other arithmetic: 113 us -> 0 us
  matrix products: 77.1 us -> 0 us
  starting transfers between devices: 9.25 us -> 0 us
  loops' own time: 0.14 us -> 8.06 us
    psum x2 -> x0, waiting for transfers between devices: 158 us -> none  [the longest x1 87.9 us: shards(): cross = lax.psum(jnp.dot(front_scaled.T, cov_below, precision=exact), 'row')]
    pallas_call x0 -> x2, Pallas kernels: none -> 131 us  [the longest x1 127 us: fast(): pl.pallas_call(work, out_shape=[shape((768, 128)), shape((1024, 128))], i...]
    another operation x3 -> x0, other arithmetic: 83.3 us -> none  [solve_right(): jax.scipy.linalg.solve_triangular(factor, rows.T, lower=True, trans=1)]
    all_to_all x1 -> x0, waiting for transfers between devices: 68.1 us -> none  [shards(): lax.all_to_all(outgoing, 'row', split_axis=0, concat_axis=0, tiled=True)]
    gather x8 -> x0, local copies, waits for them, and re-layouts: 55.5 us -> none  [the longest x3 35.9 us: shards(): jnp.take(tiled, col_tiles, axis=1)]
    another operation x45 -> x0, matrix products: 53.5 us -> none  [the longest x15 29.5 us: solve_right(): jax.scipy.linalg.solve_triangular(factor, rows.T, lower=True, trans=1)]
    unnamed x47 -> x2, local copies, waits for them, and re-layouts: 25.3 us -> 1.54 us
    dot_general x2 -> x0, matrix products: 23.7 us -> none  [the longest x1 18.4 us: shards(): row_terms = jnp.dot(front_tiles, scaled, precision=exact)]
  transfers between devices with their start and end apart: 5 -> 0, of which waited for: 4 -> 0; matrix products, arithmetic and copies ran while one was open for 48% -> 0% of each run, Pallas kernels for 0% -> 0%
where the time goes in v2:
time: 156 us
  Pallas kernels  131 us (84%)
  between operations  14.7 us (9%)
  loops' own time  8.06 us (5%)
  local copies, waits for them, and re-layouts  2.12 us (1%)
    pallas_call x1, Pallas kernels, fast(): pl.pallas_call(work, out_shape=[shape((768, 128)), shape((1024, 128))], i...  127 us
    another operation x1, loops' own time, shards(): lax.cond(table[OVER] == 0, fast, general, ancestor_inv, update_tiles, til...  8.06 us
    pallas_call x1, Pallas kernels, shards(): pl.pallas_call(tables, out_shape=shape((64,), jnp.int32), in_specs=[SMEM,...  3.66 us

profile of v2, /device:TPU:6, one launch (start us, length us, event | category | flops | bytes accessed | tf_op | source)
XLA Modules:
  0.0 155.7 jit_solution(9312342478961133321)
XLA Ops:
  7.2 3.7 %tables.1 = s32[64]{0:T(128)S(1)} custom-call(s32[96]{0:T(128)} %upd.1, s32[192]{0:T(256)} %slots.1), custom_call_target="tpu_custom_call" | custom-call | tf_op jit(solution)/shard_map/tables/pallas_call | solution.py:627
  10.8 0.6 slice.210
  12.1 135.2 %conditional.1 = ((f32[768,128]{1,0:T(8,128)S(1)}, f32[1024,128]{1,0:T(8,128)S(1)})) conditional(s32[]{:T(128)} %bitcast.19, (s32[96]{0:T(128)}, s32[192]{0:T(256)}, f32[1536,3072]{1,0:T(8,128)}, f32[1024,1024]{1,0:T(8,128)}, f32[1536,64]{0,1:T(8,128)}) %tuple.15, (f32[1536,3072]{1,0:T(8,128)}, f32[1536,64]{0,1:T(8,128)}, s32[64]{0:T(128)S(1)}, ...), branch_computations={%region_0.8_spmd, %region_7.9_spmd} | conditional | flops 28407451648 | bytes 473358720 | solution.py:660
  19.9 127.2 %work.1 = (f32[768,128]{1,0:T(8,128)S(1)}, f32[1024,128]{1,0:T(8,128)S(1)}) custom-call(s32[64]{0:T(128)S(1)} %get-tuple-element.24.table, f32[12,128,3072]{2,1,0:T(8,128)} %bitcast.132, f32[64,1536]{1,0:T(8,128)} %bitcast.143, f32[1024,1024]{1,0:T(8,128)} %get-tuple-element.27.diag), custom_call_target="tpu_custom_call" | custom-call | tf_op jit(solution)/shard_map/cond/branch_1_fun/work/pallas_call | solution.py:639
  147.3 0.7 copy.93
  148.1 0.8 copy.94

commit v3 on v2

--- a/solution.py
+++ b/solution.py
@@ -15,79 +15,8 @@
 SMEM = pl.BlockSpec(memory_space=pltpu.SMEM)
 ANY = pl.BlockSpec(memory_space=pl.ANY)
 LIMIT = 60 * 1024 * 1024
-ROWS, COLS, SLOT, FROM, OVER = 0, 8, 20, 36, 42
+ROWS, COLS, SLOT, FROM, KEEP, TURN = 0, 8, 20, 36, 42, 48
 FULL, LOW, HIGH = (0, 32), (0, 16), (16, 16)
-
-
-def spread(value, axis, root):
-    mine = lax.axis_index(axis) == root
-    return lax.psum(jnp.where(mine, value, jnp.zeros_like(value)), axis)
-
-
-def solve_right(rows, factor):
-    return jax.scipy.linalg.solve_triangular(factor, rows.T, lower=True, trans=1).T
-
-
-def general(ancestor_inv, update_tiles, tile_slot, lower_below, diag_factor):
-    rows_count = lax.axis_size("row")
-    cols_count = lax.axis_size("col")
-    this_row = lax.axis_index("row")
-    this_col = lax.axis_index("col")
-    share_rows = UTILES // rows_count
-    share_cols = UTILES // cols_count
-    slots_dev = ATILES // rows_count
-    block_cols = ATILES // cols_count
-    capacity = (share_rows + rows_count - 1) // rows_count
-    narrow = JW // cols_count
-    exact = lax.Precision.HIGHEST
-    gathered = lax.all_gather(lower_below, "row", axis=1, tiled=True)
-    scaled = solve_right(gathered, diag_factor)
-    positions = jnp.arange(UTILES, dtype=jnp.int32)
-    slot_of = jnp.take(tile_slot, update_tiles)
-    owner_of = slot_of // slots_dev
-    target_of = positions // share_rows
-    same_group = (
-        (owner_of[:, None] == owner_of[None, :])
-        & (target_of[:, None] == target_of[None, :])
-        & (positions[None, :] < positions[:, None])
-    )
-    rank_of = jnp.sum(same_group.astype(jnp.int32), axis=1)
-    send_slots = jnp.arange(rows_count * capacity, dtype=jnp.int32)
-    target_ids = send_slots // capacity
-    rank_ids = send_slots % capacity
-    matches = (
-        (target_of[None, :] == target_ids[:, None])
-        & (owner_of[None, :] == this_row)
-        & (rank_of[None, :] == rank_ids[:, None])
-    )
-    local_slot = jnp.sum(jnp.where(matches, slot_of[None, :] - this_row * slots_dev, 0), axis=1)
-    present = jnp.any(matches, axis=1).astype(jnp.float32)
-    col_tiles = (
-        lax.dynamic_slice_in_dim(update_tiles, this_col * share_cols, share_cols)
-        - this_col * block_cols
-    )
-    tiled = ancestor_inv.reshape(slots_dev * TILE, block_cols, TILE)
-    local_cols = jnp.take(tiled, col_tiles, axis=1).reshape(slots_dev, TILE, share_cols * TILE)
-    own_positions = lax.dynamic_slice_in_dim(positions, this_row * share_rows, share_rows)
-    arrival = jnp.take(owner_of, own_positions) * capacity + jnp.take(rank_of, own_positions)
-    outgoing = jnp.take(local_cols, local_slot, axis=0) * present[:, None, None]
-    incoming = lax.all_to_all(outgoing, "row", split_axis=0, concat_axis=0, tiled=True)
-    front_tiles = jnp.take(incoming, arrival, axis=0).reshape(share_rows * TILE, share_cols * TILE)
-    row_terms = jnp.dot(front_tiles, scaled, precision=exact)
-    cov_below = -lax.psum_scatter(row_terms, "col", scatter_dimension=1, tiled=True)
-    root = this_row * share_rows // share_cols
-    start = this_row * share_rows % share_cols * TILE
-    own_scaled = lax.dynamic_slice_in_dim(scaled, start, share_rows * TILE, 0)
-    front_scaled = spread(own_scaled, "col", root)
-    columns = (
-        jnp.arange(JW, dtype=jnp.int32)[:, None]
-        == this_col * narrow + jnp.arange(narrow, dtype=jnp.int32)[None, :]
-    ).astype(jnp.float32)
-    half_solve = jax.scipy.linalg.solve_triangular(diag_factor, columns, lower=True)
-    diag_inverse = jax.scipy.linalg.solve_triangular(diag_factor, half_solve, lower=True, trans=1)
-    cross = lax.psum(jnp.dot(front_scaled.T, cov_below, precision=exact), "row")
-    cov_diag = diag_inverse - cross
-    return (cov_below, cov_diag)
 
 
 def split(value):
@@ -107,42 +36,59 @@
     )
 
 
-def greet(peers):
+def greet(peers, more, far, extra):
     barrier = pltpu.get_barrier_semaphore()
     for peer in peers:
         pl.semaphore_signal(barrier, inc=1, device_id=peer, device_id_type=MESH)
-    pl.semaphore_wait(barrier, len(peers))
-
-
-def tables(upd, slots, table, counts):
+
+    @pl.when(more)
+    def _():
+        pl.semaphore_signal(barrier, inc=1, device_id=far, device_id_type=MESH)
+
+    pl.semaphore_wait(barrier, len(peers) + extra)
+
+
+def tables(upd, slots, first, second, more, counts):
     row, col = lax.axis_index("row"), lax.axis_index("col")
-    for i in range(64):
-        table[i] = 0
+    more[0] = 0
     for i in range(16):
         counts[i] = 0
+    for turn, table in enumerate((first, second)):
+        for i in range(48):
+            table[i] = 0
+        for k in range(12):
+            table[COLS + k] = upd[12 * col + k] - 24 * col
+        table[TURN] = turn
 
     def visit(u, carry):
         slot = slots[upd[u]]
         owner = slot // 12
         seen = counts[owner]
         counts[owner] = seen + 1
+        target = u // 6
 
         @pl.when(seen >= 6)
         def _():
-            table[OVER] = 1
-
-        @pl.when((owner == row) & (seen < 6))
-        def _():
-            table[ROWS + seen] = slot - 12 * row
-            table[SLOT + u // 6] = seen
+            more[0] = 1
+
+        @pl.when(owner == row)
+        def _():
+            for turn, table in enumerate((first, second)):
+
+                @pl.when(seen // 6 == turn)
+                def _():
+                    table[ROWS + seen - 6 * turn] = slot - 12 * row
+                    table[SLOT + target] = seen - 6 * turn
+
+        @pl.when(target == row)
+        def _():
+            for turn, table in enumerate((first, second)):
+                table[FROM + u - 6 * row] = owner
+                table[KEEP + u - 6 * row] = jnp.where(seen // 6 == turn, 1, 0)
 
         return carry
 
     lax.fori_loop(0, UTILES, visit, 0)
-    for k in range(12):
-        table[COLS + k] = upd[12 * col + k] - 24 * col
-    for i in range(6):
-        table[FROM + i] = slots[upd[6 * row + i]] // 12
 
 
 ITEMS = (
@@ -154,8 +100,8 @@
 def work(
     table, anc, lbt, diag, cov, cov_diag,
     ancv, bg, sh, sl, bh, bl, ph, pq, qr, d2r, d1r, brx, dg, inv, lh, ll,
-    co, slots, inc, wp, wr, wall, ch, cl,
-    anc_sem, own_sem, dg_sem, gs, gr, xs, ps, sr, es, er, rs, rr, is_, ir, as_, ar, bs, br, cs, cr,
+    co, slots, inc, wp, w1, s1, w2, g1, wall, ch, cl,
+    anc_sem, own_sem, dg_sem, gs, gr, xs, sr, ss, sg, ps, pr, es, er, rs, rr, is_, ir, as_, ar, bs, br,
 ):
     row, col = lax.axis_index("row"), lax.axis_index("col")
     y, z, x, core = row // 4, row % 4, col // 2, col % 2
@@ -179,7 +125,15 @@
         load.start()
     peers = [lax.rem(row + d, 16) for d in range(1, 16)]
     origins = [lax.rem(row + 16 - d, 16) for d in range(1, 16)]
-    greet([(peer, col) for peer in peers] + [(row, along(1)), (row, along(-1)), (row, other)])
+    parity = row % 2
+    root_x, root_core = row // 4, (row // 2) % 2
+    dist = lax.rem(x - root_x + 4, 4)
+    ring = core == root_core
+    opposite = jnp.where(ring & (dist != 2), 1, 0)
+    greet(
+        [(peer, col) for peer in peers] + [(row, along(1)), (row, along(-1)), (row, other)],
+        ring & (dist != 0), (row, along(2)), opposite,
+    )
     own.wait()
 
     def rel(h, a, b):
@@ -225,75 +179,87 @@
         for got in arr[h, a, b]:
             got.wait_recv()
 
-    parity = row % 2
-    root_x, root_core = row // 4, (row // 2) % 2
-    dist = lax.rem(x - root_x + 4, 4)
-    ring = core == root_core
-
-    def spread_copies(i):
-        def make(h, device):
-            view = brx.at[i, pl.ds(32 * h, 32)]
-            return remote(view, view, xs.at[i, h], sr.at[i, h], row, device)
-
-        def partner(h):
-            view = brx.at[i, pl.ds(32 * h, 32)]
-            return remote(view, view, ps.at[i, h], sr.at[i, h], row, other)
-
-        return make(0, along(1)), make(1, along(-1)), partner(0), partner(1)
-
-    def spread_root(i):
+    def quarter(d):
+        return pl.ds(pl.multiple_of(16 * d, 16), 16)
+
+    def chip(d):
+        return 2 * lax.rem(root_x + d, 4) + root_core
+
+    def scatter_copy(i, d):
+        view = brx.at[i, quarter(d)]
+        return remote(view, view, xs.at[i, d - 1], sr.at[i], row, chip(d))
+
+    def scatter(i):
         @pl.when(ring & (dist == 0))
         def _():
             lanes = pl.ds(pl.multiple_of(768 * parity, 768), 768)
             for h in range(2):
                 brx[i, pl.ds(32 * h, 32), :] = bg[rel(h, *ITEMS[i]), pl.ds(32 * h, 32), lanes]
-            for copy in spread_copies(i):
-                copy.start()
-
-    def spread_hop(i, hop):
-        up, down, pup, pdown = spread_copies(i)
-
-        @pl.when(ring & (dist == hop))
-        def _():
-            up.wait_recv()
-            if hop < 3:
-                up.start()
-            pup.start()
-
-        @pl.when(ring & (dist == 4 - hop))
-        def _():
-            down.wait_recv()
-            if hop < 3:
-                down.start()
-            pdown.start()
-
-    def spread_end(i):
-        up, down, pup, pdown = spread_copies(i)
+            for d in (1, 2, 3):
+                scatter_copy(i, d).start()
+
+    def batch(b):
+        return pl.ds(8 * b, 8)
+
+    def share_copy(b, e):
+        view = brx.at[batch(b), quarter(dist)]
+        return remote(view, view, ss.at[b, e - 1], sg.at[b, e - 1], row, along(e))
+
+    def share(b):
+        for i in range(8 * b, 8 * b + 8):
+
+            @pl.when(ring & (dist != 0))
+            def _():
+                view = brx.at[i, quarter(dist)]
+                remote(view, view, xs.at[i, 0], sr.at[i], row, along(1)).wait_recv()
+
+        for e in (1, 3, 2):
+
+            @pl.when(ring & (lax.rem(dist + e, 4) != 0))
+            def _():
+                share_copy(b, e).start()
+
+    def partner_copy(b):
+        view = brx.at[batch(b)]
+        return remote(view, view, ps.at[b], pr.at[b], row, other)
+
+    def hand_over(b):
+        @pl.when(ring & (dist != 0))
+        def _():
+            for e in (1, 2, 3):
+                view = brx.at[batch(b), quarter(lax.rem(dist - e + 4, 4))]
+                remote(view, view, ss.at[b, e - 1], sg.at[b, e - 1], row, along(e)).wait_recv()
 
         @pl.when(ring)
         def _():
-            pup.wait_send()
-            pdown.wait_send()
-
-            @pl.when(dist != 3)
+            partner_copy(b).start()
+
+    def spread_end(b):
+        @pl.when(jnp.logical_not(ring))
+        def _():
+            partner_copy(b).wait_recv()
+
+    def spread_sent():
+        for b in range(2):
+
+            @pl.when(ring)
             def _():
-                up.wait_send()
-
-            @pl.when(dist != 1)
-            def _():
-                down.wait_send()
-
-        @pl.when(jnp.logical_not(ring))
-        def _():
-            pup.wait_recv()
-            pdown.wait_recv()
+                partner_copy(b).wait_send()
+
+            for e in (1, 2, 3):
+
+                @pl.when(ring & (lax.rem(dist + e, 4) != 0))
+                def _():
+                    share_copy(b, e).wait_send()
+
+        @pl.when(ring & (dist == 0))
+        def _():
+            for i in range(16):
+                for d in (1, 2, 3):
+                    scatter_copy(i, d).wait_send()
 
     def spread_step(i):
-        if i < 16:
-            spread_root(i)
-        for hop in (1, 2, 3):
-            if 0 <= i - hop < 16:
-                spread_hop(i - hop, hop)
+        scatter(i)
 
     def extract(j, carry):
         for k in range(12):
@@ -456,6 +422,7 @@
     spread_step(11)
     spread_step(12)
     group(2)
+    share(0)
     for h in both:
         wait(h, 2, -1)
         wait(h, 2, 1)
@@ -545,7 +512,6 @@
     columns(0, 3)
     merged(0, 2)
     near_down(0)
-    spread_step(16)
     product(3, 1)
     merged(0, 3)
     columns(1, 0)
@@ -560,16 +526,17 @@
     merged(1, 2)
     near_down(1)
     merged(1, 3)
-    spread_step(17)
+    hand_over(0)
     finish(0)
     passed(1)
-    spread_step(18)
-    for i in range(16):
-        spread_end(i)
+    share(1)
     for m in range(8):
         s = pl.ds(128 * m, 128)
         lh[:, s], ll[:, s] = split(inv[s, :].T)
     finish(1)
+    hand_over(1)
+    spread_end(0)
+    spread_end(1)
 
     for chunk in range(2):
         for k in range(15):
@@ -578,6 +545,7 @@
     for i in range(6):
         for half in range(2):
             tile = inc[half, table[FROM + i]]
+            tile = jnp.where(jnp.full((64, 128), table[KEEP + i]) == 1, tile, 0.0)
             r = pl.ds(128 * i + 64 * half, 64)
             cov[r, :] = tile
             ch[r, :], cl[r, :] = split(tile)
@@ -586,37 +554,69 @@
         part = dot3(*split(rows), ch[pl.ds(0, 768), :], cl[pl.ds(0, 768), :])
         for i in range(4):
             for h in range(2):
-                dst = pl.ds(pl.multiple_of(64 * rel(h, *ITEMS[4 * m + i]) + 32 * h, 32), 32)
-                wp[dst, :] = part[64 * i + 32 * h : 64 * i + 32 * h + 32]
-    parts = []
-    for k, peer in enumerate(peers):
-        src = wp.at[pl.ds(pl.multiple_of(peer * 64, 64), 64)]
-        copy = remote(src, wr.at[row], bs.at[k], br.at[k], peer, col)
+                place = rel(h, *ITEMS[4 * m + i])
+                wp[place // 4, place % 4, h] = part[64 * i + 32 * h : 64 * i + 32 * h + 32]
+    steps = {}
+
+    def step_to(h, axis, d):
+        return at(0, d) if axis == 0 else at(d, 0)
+
+    def exchange(stage, h, d, axis, src, dst, mine):
+        copy = remote(src, dst, bs.at[stage, h, d - 1], br.at[stage, h, d - 1], step_to(h, axis, d), col)
         copy.start()
-        parts.append(copy)
-    here = pl.ds(pl.multiple_of(row * 64, 64), 64)
-    total = inv[here, pl.ds(pl.multiple_of(col * 128, 128), 128)] - wp[here, :]
-    for k in range(15):
-        mine = wr.at[origins[k]]
-        remote(mine, mine, bs.at[k], br.at[k], peers[k], col).wait_recv()
-        total -= wr[origins[k]]
-    wall[row] = total
-    ends = []
-    for k, peer in enumerate(peers):
-        copy = remote(wall.at[row], wall.at[row], cs.at[k], cr.at[k], peer, col)
-        copy.start()
-        ends.append(copy)
-    for k in range(15):
-        mine = wall.at[origins[k]]
-        remote(mine, mine, cs.at[k], cr.at[k], peers[k], col).wait_recv()
+        got = remote(mine, mine, bs.at[stage, h, d - 1], br.at[stage, h, d - 1], step_to(h, axis, d), col)
+        steps[stage, h, d] = (copy, got)
+
+    DS = (1, 3, 2)
+    for d in DS:
+        zd, yd = lax.rem(z + d, 4), lax.rem(y + d, 4)
+        exchange(0, 0, d, 0, wp.at[:, zd, 0], w1.at[0, d - 1], w1.at[0, d - 1])
+        exchange(0, 1, d, 1, wp.at[yd, :, 1], w1.at[1, d - 1], w1.at[1, d - 1])
+    for h in both:
+        value = wp[:, z, 0] if h == 0 else wp[y, :, 1]
+        for d in DS:
+            steps[0, h, d][1].wait_recv()
+            value += w1[h, d - 1]
+        s1[h] = value
+        for d in DS:
+            there = lax.rem((y if h == 0 else z) + d, 4)
+            exchange(1, h, d, 1 - h, s1.at[h, there], w2.at[h, d - 1], w2.at[h, d - 1])
+    for h in both:
+        place = y if h == 0 else z
+        here = pl.ds(pl.multiple_of(row * 64 + 32 * h, 32), 32)
+        value = inv[here, pl.ds(pl.multiple_of(col * 128, 128), 128)]
+        value = jnp.where(jnp.full((32, 128), table[TURN]) == 0, value, 0.0) - s1[h, place]
+        for d in DS:
+            steps[1, h, d][1].wait_recv()
+            value -= w2[h, d - 1]
+        g1[h, place] = value
+        for d in DS:
+            back = lax.rem(place + 4 - d, 4)
+            exchange(2, h, d, 1 - h, g1.at[h, place], g1.at[h, place], g1.at[h, back])
+    for h in both:
+        for d in DS:
+            steps[2, h, d][1].wait_recv()
+        if h == 0:
+            wall[:, z, 0] = g1[0]
+        else:
+            wall[y, :, 1] = g1[1]
+        for d in DS:
+            if h == 0:
+                exchange(3, h, d, 0, g1.at[0], wall.at[:, z, 0], wall.at[:, lax.rem(z + 4 - d, 4), 0])
+            else:
+                exchange(3, h, d, 1, g1.at[1], wall.at[y, :, 1], wall.at[lax.rem(y + 4 - d, 4), :, 1])
+    for h in both:
+        for d in DS:
+            steps[3, h, d][1].wait_recv()
     ch[...], cl[...] = split(wall[...].reshape(1024, 128))
     for m in range(4):
         r = pl.ds(256 * m, 256)
         cov_diag[r, :] = dot3(lh[r, :], ll[r, :], ch[...], cl[...])
     for copy in sends + swap_inv + list(swaps.values()) + list(moves.values()) + list(tile_copies.values()):
         copy.wait_send()
-    for copy in parts + ends:
+    for copy, _ in steps.values():
         copy.wait_send()
+    spread_sent()
 
 
 def shape(dims, dtype=F32):
@@ -624,18 +624,19 @@
 
 
 def shards(ancestor_inv, update_tiles, tile_slot, lower_below, diag_factor):
-    table = pl.pallas_call(
+    vm = pltpu.VMEM
+    dma = pltpu.SemaphoreType.DMA
+
+    first, second, more = pl.pallas_call(
         tables,
-        out_shape=shape((64,), jnp.int32),
+        out_shape=[shape((64,), jnp.int32), shape((64,), jnp.int32), shape((1,), jnp.int32)],
         in_specs=[SMEM, SMEM],
-        out_specs=SMEM,
+        out_specs=[SMEM] * 3,
         scratch_shapes=[pltpu.SMEM((16,), jnp.int32)],
         name="tables",
     )(update_tiles, tile_slot)
 
-    def fast(ancestor_inv, update_tiles, tile_slot, lower_below, diag_factor):
-        vm = pltpu.VMEM
-        dma = pltpu.SemaphoreType.DMA
+    def call(table):
         return pl.pallas_call(
             work,
             out_shape=[shape((768, 128)), shape((1024, 128))],
@@ -647,19 +648,24 @@
                 vm((4, 6, 128, 128), F32), vm((2, 2, 3, 64, 128), F32), vm((2, 2, 3, 128, 128), F32),
                 vm((16, 64, 768), F32), vm((1024, 1024), F32), vm((1024, 1024), F32), vm((1024, 1024), BF16),
                 vm((1024, 1024), BF16), vm((2, 6, 64, 128), F32), vm((2, 16, 64, 128), F32), vm((2, 16, 64, 128), F32),
-                vm((1024, 128), F32), vm((16, 64, 128), F32), vm((16, 64, 128), F32), vm((1024, 128), BF16),
-                vm((1024, 128), BF16),
-                dma((24,)), dma(()), dma(()), dma((40,)), dma((40,)), dma((16, 2)), dma((16, 2)), dma((16, 2)),
+                vm((4, 4, 2, 32, 128), F32), vm((2, 3, 4, 32, 128), F32), vm((2, 4, 32, 128), F32),
+                vm((2, 3, 32, 128), F32), vm((2, 4, 32, 128), F32), vm((4, 4, 2, 32, 128), F32),
+                vm((1024, 128), BF16), vm((1024, 128), BF16),
+                dma((24,)), dma(()), dma(()), dma((40,)), dma((40,)), dma((16, 3)), dma((16,)), dma((2, 3)), dma((2, 3)), dma((2,)), dma((2,)),
                 dma((2, 4)), dma((2, 4)), dma((2, 6)), dma((2, 6)), dma(()), dma(()), dma((2, 15)), dma((2, 15)),
-                dma((15,)), dma((15,)), dma((15,)), dma((15,)),
+                dma((4, 2, 3)), dma((4, 2, 3)),
             ],
             compiler_params=pltpu.CompilerParams(vmem_limit_bytes=LIMIT, collective_id=0, has_side_effects=True),
             name="work",
         )(table, ancestor_inv.reshape(12, 128, 3072), lower_below.T, diag_factor)
 
-    return lax.cond(
-        table[OVER] == 0, fast, general, ancestor_inv, update_tiles, tile_slot, lower_below, diag_factor
-    )
+    cov_below, cov_diag = call(first)
+
+    def again(cov_below, cov_diag):
+        more_below, more_diag = call(second)
+        return cov_below + more_below, cov_diag + more_diag
+
+    return lax.cond(more[0] == 1, again, lambda a, b: (a, b), cov_below, cov_diag)
 
 
 def solution(mesh):

time: 156 us -> 117 us (0.75)
  Pallas kernels: 131 us -> 113 us
  between operations: 14.7 us -> 1.32 us
  loops' own time: 8.06 us -> 0.31 us
    pallas_call x2, Pallas kernels: 131 us -> 113 us  [the longest x1 108 us: call(): pl.pallas_call(work, out_shape=[shape((768, 128)), shape((1024, 128))], i...]
    another operation x1, loops' own time: 8.06 us -> 0.31 us  [shards(): lax.cond(more[0] == 1, again, lambda a, b: (a, b), cov_below, cov_diag)]
where the time goes in v3:
time: 117 us; the launch traced here: 116 us
  Pallas kernels  113 us (97%)
  local copies, waits for them, and re-layouts  1.55 us (1%)
  between operations  1.32 us (1%)
    pallas_call x1, Pallas kernels, call(): pl.pallas_call(work, out_shape=[shape((768, 128)), shape((1024, 128))], i...  108 us
    pallas_call x1, Pallas kernels, shards(): pl.pallas_call(tables, out_shape=[shape((64,), jnp.int32), shape((64,), j...  5.1 us

profile of v3, /device:TPU:6, one launch (start us, length us, event | category | flops | bytes accessed | tf_op | source)
XLA Modules:
  0.0 115.9 jit_solution(13013393477491650387)
XLA Ops:
  0.6 0.0 copy-start
  0.6 5.1 %tables.1 = (s32[64]{0:T(128)}, s32[64]{0:T(128)S(1)}, s32[1]{0:T(128)}) custom-call(s32[96]{0:T(128)} %upd.1, s32[192]{0:T(256)} %slots.1), custom_call_target="tpu_custom_call" | custom-call | tf_op jit(solution)/shard_map/tables/pallas_call | solution.py:630
  6.4 107.6 %work.3 = (f32[768,128]{1,0:T(8,128)S(1)}, f32[1024,128]{1,0:T(8,128)S(1)}) custom-call(s32[64]{0:T(128)} %get-tuple-element.32.table, f32[12,128,3072]{2,1,0:T(8,128)} %bitcast.5, f32[64,1536]{1,0:T(8,128)} %bitcast.7, f32[1024,1024]{1,0:T(8,128)} %diag.1), custom_call_target="tpu_custom_call" | custom-call | tf_op jit(solution)/shard_map/work/pallas_call | solution.py:640
  114.0 0.0 copy-done
  114.0 0.3 conditional.1
  114.3 0.7 copy.17
  115.1 0.8 copy.18
Async XLA Ops:
  0.6 113.4 %copy-start = (f32[1536,64]{0,1:T(8,128)S(1)}, f32[1536,64]{0,1:T(8,128)}, u32[]{:S(2)}) copy-start(f32[1536,64]{0,1:T(8,128)} %param.10) | copy-start | bytes 1179652
